TPU v7x, 256 devices: a whole 4x4x8 slice. The times are simulated.
256 devices in a mesh: dp: 4 (over x), cent: 64 (over z, y, core).
Axes of the slice: x: 4, y: 4, z: 8, core: 2. Of those that a mesh axis runs over, the one named last changes fastest.
Arguments:
- embeddings: bfloat16 [8192, 1024], P('dp'), may hold values from -64 to 64
- centroids: bfloat16 [32768, 1024], P('cent'), may hold values from -2 to 2
Outputs:
- new_centroids: float32 [32768, 1024], P('cent', 'dp')
- log_totals: float32 [8192], P('dp')
All inputs are finite; a program needn't handle non-finite values.
Results may differ from a plain program's by a relative error of at most 0.012.
Values may be sent and summed in bfloat16 or wider, within the bound.
No kernel may reach another device: no remote copies, remote signals or barrier semaphores. Data moves between devices by JAX's collectives and lax.ppermute only.
A program may use at most 64 MiB of HBM per device.

v0:
```python
import math

import jax
import jax.numpy as jnp
from jax import lax
from jax.sharding import PartitionSpec as P

BLOCK = 512


softness_level = 0.1
prior_mass = 4.0


def block_logits(embedding_row_tile, centroids, squared_norms):
    inner_products = lax.dot_general(
        embedding_row_tile, centroids, (((1,), (1,)), ((), ())), preferred_element_type=jnp.float32
    )
    return (2.0 * inner_products - squared_norms[None, :]) / (
        softness_level * math.sqrt(embedding_row_tile.shape[1])
    )


def merge_stats(logits):
    shard_peak_logit = jnp.max(logits, axis=1)
    local_sum = jnp.sum(jnp.exp(logits - shard_peak_logit[:, None]), axis=1)
    row_top = lax.pmax(shard_peak_logit, "cent")
    sum_total = lax.psum(local_sum * jnp.exp(shard_peak_logit - row_top), "cent")
    return row_top + jnp.log(sum_total)


def accumulate(embedding_row_tile, logits, log_total, numerator, mass_sum):
    weights = jnp.exp(logits - log_total[:, None]).astype(jnp.bfloat16)
    numerator = numerator + lax.dot_general(
        weights, embedding_row_tile, (((0,), (0,)), ((), ())), preferred_element_type=jnp.float32
    )
    mass_sum = mass_sum + jnp.sum(weights.astype(jnp.float32), axis=0)
    return (numerator, mass_sum)


def shards(embeddings, centroids):
    row_count = embeddings.shape[0]
    feature_width = embeddings.shape[1]
    cent_count = centroids.shape[0]
    cent_f = centroids.astype(jnp.float32)
    squared_norms = jnp.sum(cent_f * cent_f, axis=1)
    step_rows = min(BLOCK, row_count)
    numerator = jnp.zeros((cent_count, feature_width), jnp.float32)
    mass_sum = jnp.zeros((cent_count,), jnp.float32)
    lse_pieces = []
    for first_row in range(0, row_count, step_rows):
        embedding_row_tile = embeddings[first_row : first_row + step_rows]
        logits = block_logits(embedding_row_tile, centroids, squared_norms)
        log_total = merge_stats(logits)
        numerator, mass_sum = accumulate(embedding_row_tile, logits, log_total, numerator, mass_sum)
        lse_pieces.append(log_total)
    lse_all = jnp.concatenate(lse_pieces)
    col_span = feature_width // lax.axis_size("dp")
    col_offset = lax.axis_index("dp") * col_span
    numer_all, mass_all = (
        lax.psum(numerator.astype(jnp.bfloat16), "dp").astype(jnp.float32),
        lax.psum(mass_sum.astype(jnp.bfloat16), "dp").astype(jnp.float32),
    )
    numer_own = lax.dynamic_slice_in_dim(numer_all, col_offset, col_span, 1)
    prior_own = lax.dynamic_slice_in_dim(cent_f, col_offset, col_span, 1)
    new_centroids = (numer_own + prior_mass * prior_own) / (mass_all[:, None] + prior_mass)
    return (new_centroids, lse_all)


def solution(mesh):
    in_specs = (P("dp", None), P("cent", None))
    out_specs = (P("cent", "dp"), P("dp"))
    return jax.shard_map(shards, mesh=mesh, in_specs=in_specs, out_specs=out_specs, check_vma=False)
```

profile of v0, /device:TPU:38, one launch (start us, length us, event | category | flops | bytes accessed | tf_op | source)
XLA Modules:
  0.0 333.8 jit_solution(16323806366629650310)
XLA Ops:
  7.2 0.0 copy-start.1
  7.2 0.0 all-reduce.4.cloned.1.call-start
  7.2 0.0 copy-start.3
  7.2 1.7 multiply_reduce_fusion
  8.9 2.4 fusion.19
  11.3 0.0 copy-done.1
  11.4 0.0 copy-done.3
  11.4 0.0 copy-start.2
  11.4 0.8 fusion.20
  12.1 0.8 fusion.21
  12.9 0.0 copy-done.2
  12.9 0.0 copy-start
  12.9 0.8 fusion.22
  13.7 0.2 exponential_reduce_fusion
  13.9 0.0 copy-done
  13.9 0.2 exponential_reduce_fusion.2
  14.1 115.5 %all-reduce.1 = (f32[512]{0:T(512)S(1)}, f32[512]{0:T(512)S(1)}, f32[512]{0:T(512)S(1)}, f32[512]{0:T(512)S(1)}) all-reduce(f32[512]{0:T(512)S(1)} %get-tuple-element.10, f32[512]{0:T(512)S(1)} %get-tuple-element.12, f32[512]{0:T(512)S(1)} %get-tuple-element.14, f32[512]{0:T(512)S(1)} %get-tuple-element.16), channel_id=1, replica_groups=mesh['dp'=4,'cent'=64] {'cent'}, use_global_device_ids=true, to_apply=%region_10.0 | all-reduce | flops 2048 | bytes 16384 | tf_op jit(solution)/shard_map/pmax | solution.py:27
  129.6 0.2 exponential_reduce_fusion.3
  129.8 0.2 exponential_reduce_fusion.1
  130.1 126.1 %all-reduce = (f32[512]{0:T(512)S(1)}, f32[512]{0:T(512)S(1)}, f32[512]{0:T(512)S(1)}, f32[512]{0:T(512)S(1)}) all-reduce(f32[512]{0:T(512)S(1)} %exponential_multiply_fusion.1, f32[512]{0:T(512)S(1)} %exponential_multiply_fusion.3, f32[512]{0:T(512)S(1)} %exponential_multiply_fusion.2, ...), channel_id=1, replica_groups=mesh['dp'=4,'cent'=64] {'cent'}, use_global_device_ids=true, to_apply=%region_12.0 | all-reduce | flops 2048 | bytes 16384 | tf_op jit(solution)/shard_map/psum | solution.py:28
  256.1 0.0 copy-start.4
  256.2 2.4 fusion.13
  258.6 0.4 copy-done.4
  259.0 0.7 fusion.16
  259.7 0.7 fusion.10
  260.4 1.8 add_convert_fusion
  262.2 0.0 all-reduce.4.cloned.1.call-update
  262.2 1.5 convert_reduce_fusion.2
  263.7 2.8 convert_element_type.39
  266.5 0.2 convert_reduce_fusion.3
  266.7 0.2 convert_reduce_fusion
  266.9 0.2 convert_reduce_fusion.1
  267.2 7.5 %psum.47 = bf16[512]{0:T(512)(128)(2,1)S(1)} all-reduce(bf16[512]{0:T(512)(128)(2,1)S(1)} %add_convert_fusion.1), channel_id=1, replica_groups=mesh['dp'=4,'cent'=64] {'dp'}, use_global_device_ids=true, to_apply=%region_22.0 | all-reduce | flops 512 | bytes 2048 | tf_op jit(solution)/shard_map/psum | solution.py:62
  274.7 0.6 pad_maximum_fusion
  275.3 49.7 %all-reduce.4.cloned.1.call-done = bf16[512,1024]{1,0:T(8,128)(2,1)} async-done(((bf16[512,1024]{1,0:T(8,128)(2,1)}), bf16[512,1024]{1,0:T(8,128)(2,1)}) %all-reduce.4.cloned.1.call-update) | async-done | bytes 1048592 | tf_op jit(solution)/shard_map/psum | solution.py:61
  324.9 2.0 add_divide_fusion
  (8 shorter events, 0.1 us)
Async XLA Ops:
  7.2 4.2 %copy-start.1 = (bf16[512,1024]{1,0:T(8,128)(2,1)S(1)}, bf16[512,1024]{1,0:T(8,128)(2,1)}, u32[]{:S(2)}) copy-start(bf16[512,1024]{1,0:T(8,128)(2,1)} %param.3) | copy-start | bytes 3145732
  7.2 317.8 %all-reduce.4.cloned.1.call-start = ((), (), s32[]{:S(2)}) async-start(), calls=%async_computation | async-start | bytes 2097152 | tf_op jit(solution)/shard_map/psum | solution.py:61
  7.2 4.1 %copy-start.3 = (bf16[2048,1024]{1,0:T(8,128)(2,1)S(1)}, bf16[2048,1024]{1,0:T(8,128)(2,1)}, u32[]{:S(2)}) copy-start(bf16[2048,1024]{1,0:T(8,128)(2,1)} %param.2) | copy-start | bytes 12582916
  11.4 1.5 copy-start.2
  12.9 1.0 copy-start
  256.1 2.8 copy-start.4
Sparse Core Ops, SparseCore 0:
  262.3 62.5 all-reduce.3
where the time goes:
time: 335 us; the launch traced here: 334 us
  blocking collectives  249 us (74%)
  waiting for transfers between devices  49.7 us (15%)
  between operations  14.2 us (4%)
  matrix products  10.3 us (3%)
  other arithmetic  10.1 us (3%)
    psum x1, blocking collectives, merge_stats(): lax.psum(local_sum * jnp.exp(shard_peak_logit - row_top), 'cent')  126 us
    pmax x1, blocking collectives, merge_stats(): row_top = lax.pmax(shard_peak_logit, 'cent')  116 us
    psum x1, waiting for transfers between devices, shards(): lax.psum(numerator.astype(jnp.bfloat16), 'dp').astype(jnp.float32)  49.7 us
    psum x1, blocking collectives, shards(): lax.psum(mass_sum.astype(jnp.bfloat16), 'dp').astype(jnp.float32)  7.49 us
  transfers between devices with their start and end apart: 1, of which 1 were waited for; matrix products, arithmetic and copies ran while one was open for 2% of the time, Pallas kernels for 0%

commit v1 on v0

v1 whole, which is shorter than its diff:
```python
import functools
import math

import jax
import jax.numpy as jnp
from jax import lax
from jax.experimental import pallas as pl
from jax.experimental.pallas import tpu as pltpu
from jax.sharding import Mesh, PartitionSpec as P

SOFTNESS = 0.1
PRIOR = 4.0
LOG2E = math.log2(math.e)
LN2 = math.log(2.0)
ROWS = 256
VMEM_LIMIT = 56 * 1024 * 1024


def logits_kernel(scale, emb_ref, cent_ref, z_ref, lse_ref, half_sq):
    step = pl.program_id(0)

    @pl.when(step == 0)
    def _():
        c = cent_ref[...].astype(jnp.float32)
        half_sq[...] = 0.5 * jnp.sum(c * c, axis=1, keepdims=True)

    inner = lax.dot_general(
        cent_ref[...], emb_ref[...], (((1,), (1,)), ((), ())), preferred_element_type=jnp.float32
    )
    z = (inner - half_sq[...]) * scale
    z_ref[...] = z
    top = jnp.max(z, axis=0, keepdims=True)
    total = jnp.sum(jnp.exp2(z - top), axis=0, keepdims=True)
    lse = top + jnp.log2(total)
    lse_ref[...] = jnp.broadcast_to(lse, lse_ref.shape)


def weights_kernel(n_dp, z_ref, tot_ref, emb_ref, out_ref, w_ref):
    cents, rows = z_ref.shape
    cols = emb_ref.shape[1] // n_dp
    mass = jnp.zeros((cents, 128), jnp.float32)
    for r in range(rows // 128):
        w = jnp.exp2(z_ref[:, r * 128 : (r + 1) * 128] - tot_ref[r : r + 1, :]).astype(jnp.bfloat16)
        w_ref[:, r * 128 : (r + 1) * 128] = w
        mass = mass + w.astype(jnp.float32)
    mass = jnp.broadcast_to(jnp.sum(mass, axis=1, keepdims=True), (cents, 128)).T
    mass_rows = jnp.concatenate([mass[:8, :cols], mass[:8, cols:]], axis=0).astype(jnp.bfloat16)
    for d in range(n_dp):
        out_ref[d, :cents, :] = jnp.dot(
            w_ref[...], emb_ref[:, d * cols : (d + 1) * cols], preferred_element_type=jnp.float32
        ).astype(jnp.bfloat16)
        out_ref[d, cents:, :] = mass_rows


def update_kernel(parts_ref, prior_ref, out_ref):
    n_dp = parts_ref.shape[0]
    cents, cols = out_ref.shape
    total = PRIOR * prior_ref[...].astype(jnp.float32)
    mass = jnp.full((16, cols), PRIOR, jnp.float32)
    for d in range(n_dp):
        total = total + parts_ref[d, :cents, :].astype(jnp.float32)
        mass = mass + parts_ref[d, cents:, :].astype(jnp.float32)
    inv = jnp.concatenate([mass[:1, :], mass[8:9, :]], axis=1)
    inv = 1.0 / jnp.broadcast_to(inv, (128, cents)).T
    for k in range(cols // 128):
        out_ref[:, k * 128 : (k + 1) * 128] = total[:, k * 128 : (k + 1) * 128] * inv


def merge(lse):
    top = jnp.max(lse, axis=0)
    return top + jnp.log2(jnp.sum(jnp.exp2(lse - top), axis=0))


def shards(n_dp, emb, cent):
    rows, width = emb.shape
    cents = cent.shape[0]
    cols = width // n_dp
    scale = 2.0 * LOG2E / (SOFTNESS * math.sqrt(width))
    params = pltpu.CompilerParams(vmem_limit_bytes=VMEM_LIMIT)
    z, lse = pl.pallas_call(
        functools.partial(logits_kernel, scale),
        grid=(rows // ROWS,),
        in_specs=[
            pl.BlockSpec((ROWS, width), lambda i: (i, 0)),
            pl.BlockSpec((cents, width), lambda i: (0, 0)),
        ],
        out_specs=[
            pl.BlockSpec((cents, ROWS), lambda i: (0, i)),
            pl.BlockSpec((8, ROWS), lambda i: (0, i)),
        ],
        out_shape=[
            jax.ShapeDtypeStruct((cents, rows), jnp.float32),
            jax.ShapeDtypeStruct((8, rows), jnp.float32),
        ],
        scratch_shapes=[pltpu.VMEM((cents, 1), jnp.float32)],
        compiler_params=params,
    )(emb, cent)

    core = lax.axis_index("core")
    swap = [(0, 1), (1, 0)]
    half = rows // 2
    lse = lse[0].reshape(2, half // 128, 128)
    keep = lax.dynamic_index_in_dim(lse, core, 0, keepdims=False)
    give = lax.dynamic_index_in_dim(lse, 1 - core, 0, keepdims=False)
    got = lax.ppermute(give, "core", swap)
    pair = merge(jnp.stack([keep, got]))
    peers = lax.axis_size("z") * lax.axis_size("y")
    every = lax.all_to_all(jnp.broadcast_to(pair, (peers,) + pair.shape), ("z", "y"), 0, 0)
    own_half = merge(every)
    other_half = lax.ppermute(own_half, "core", swap)
    totals = jnp.where(
        core == 0,
        jnp.concatenate([own_half, other_half]),
        jnp.concatenate([other_half, own_half]),
    )

    parts = pl.pallas_call(
        functools.partial(weights_kernel, n_dp),
        out_shape=jax.ShapeDtypeStruct((n_dp, cents + 16, cols), jnp.bfloat16),
        scratch_shapes=[pltpu.VMEM((cents, rows), jnp.bfloat16)],
        compiler_params=params,
    )(z, totals, emb)
    parts = lax.all_to_all(parts, "x", 0, 0)
    prior = lax.dynamic_slice_in_dim(cent, lax.axis_index("x") * cols, cols, 1)
    new_centroids = pl.pallas_call(
        update_kernel,
        out_shape=jax.ShapeDtypeStruct((cents, cols), jnp.float32),
        compiler_params=params,
    )(parts, prior)
    return new_centroids, (totals * LN2).reshape(rows)


def solution(mesh):
    n_dp = mesh.shape["dp"]
    fine = Mesh(mesh.devices.reshape(n_dp, 8, 4, 2), ("x", "z", "y", "core"))
    cent = ("z", "y", "core")
    return jax.shard_map(
        functools.partial(shards, n_dp),
        mesh=fine,
        in_specs=(P("x", None), P(cent, None)),
        out_specs=(P(cent, "x"), P("x")),
        check_vma=False,
    )
```

time: 335 us -> 66.5 us (0.20)
  the two profiles are of different devices: /device:TPU:38 before, /device:TPU:1 now
where the time goes in v1:
time: 66.5 us; the launch traced here: 66 us
  blocking collectives  18.6 us (28%)
  Pallas kernels  18.2 us (27%)
  waiting for transfers between devices  14.9 us (22%)
  starting transfers between devices  9.45 us (14%)
  local copies, waits for them, and re-layouts  3.53 us (5%)
  other arithmetic  0.72 us (1%)
    all_to_all x1, blocking collectives, shards(): lax.all_to_all(jnp.broadcast_to(pair, (peers,) + pair.shape), ('z', 'y'),...  18.6 us
    all_to_all x1, waiting for transfers between devices, shards(): parts = lax.all_to_all(parts, 'x', 0, 0)  13.2 us
    pallas_call x1, Pallas kernels, shards(): pl.pallas_call(functools.partial(logits_kernel, scale), grid=(rows // ROW...  8.92 us
    pallas_call x1, Pallas kernels, shards(): pl.pallas_call(functools.partial(weights_kernel, n_dp), out_shape=jax.Sha...  6.98 us
    all_to_all x1, starting transfers between devices, shards(): parts = lax.all_to_all(parts, 'x', 0, 0)  4.02 us
    ppermute x1, starting transfers between devices, shards(): got = lax.ppermute(give, 'core', swap)  3.25 us
    pallas_call x1, Pallas kernels, shards(): pl.pallas_call(update_kernel, out_shape=jax.ShapeDtypeStruct((cents, cols...  2.27 us
    ppermute x1, starting transfers between devices, shards(): other_half = lax.ppermute(own_half, 'core', swap)  2.18 us
  transfers between devices with their start and end apart: 3, of which 3 were waited for; matrix products, arithmetic and copies ran while one was open for 3% of the time, Pallas kernels for 0%

profile of v1, /device:TPU:1, one launch (start us, length us, event | category | flops | bytes accessed | tf_op | source)
XLA Modules:
  0.0 66.0 jit_solution(5538773367352251259)
XLA Ops:
  0.6 8.9 %shard_map.41 = (f32[512,2048]{1,0:T(8,128)}, f32[8,2048]{1,0:T(8,128)}) custom-call(bf16[2048,1024]{1,0:T(8,128)(2,1)} %emb_ref.3, bf16[512,1024]{1,0:T(8,128)(2,1)} %cent_ref.1), custom_call_target="tpu_custom_call" | custom-call | tf_op jit(solution)/shard_map/pallas_call | solution.py:80
  9.6 0.8 %slice.3 = f32[1,2048]{1,0:T(1,128)S(1)} slice(f32[8,2048]{1,0:T(8,128)} %get-tuple-element.5), slice={[0:1], [0:2048]} | slice | bytes 16384 | tf_op jit(solution)/shard_map/slice | solution.py:102
  10.4 3.3 %collective-permute-start = (f32[8,128]{1,0:T(8,128)S(1)}, f32[8,128]{1,0:T(8,128)S(1)}, u32[]{:S(2)}, u32[]{:S(2)}) collective-permute-start(f32[8,128]{1,0:T(8,128)S(1)} %dynamic-slice_bitcast_fusion), channel_id=1, source_target_pairs={{0,1},{1,0},{2,3},{3,2},{4,5},{5,4},{6,7},{7,6},{8,9},{9,8},{10,11... | collective-permute-start | bytes 12296 | tf_op jit(solution)/shard_map/ppermute | solution.py:105
  13.7 0.8 %collective-permute-done = f32[8,128]{1,0:T(8,128)S(1)} collective-permute-done((f32[8,128]{1,0:T(8,128)S(1)}, f32[8,128]{1,0:T(8,128)S(1)}, u32[]{:S(2)}, u32[]{:S(2)}) %collective-permute-start) | collective-permute-done | bytes 4128 | tf_op jit(solution)/shard_map/ppermute | solution.py:105
  14.5 18.6 %all_to_all.10 = f32[32,8,128]{2,1,0:T(8,128)S(1)} all-to-all(f32[32,8,128]{2,1,0:T(8,128)S(1)} %broadcast_in_dim.2), channel_id=1, replica_groups=mesh['x'=4,'z'=8,'y'=4,'core'=2] {'z','y'}, dimensions={0} | all-to-all | bytes 262144 | tf_op jit(solution)/shard_map/all_to_all | solution.py:108
  33.2 2.2 %collective-permute-start.1 = (f32[8,128]{1,0:T(8,128)S(1)}, f32[8,128]{1,0:T(8,128)S(1)}, u32[]{:S(2)}, u32[]{:S(2)}) collective-permute-start(f32[8,128]{1,0:T(8,128)S(1)} %multiply_add_fusion), channel_id=1, source_target_pairs={{0,1},{1,0},{2,3},{3,2},{4,5},{5,4},{6,7},{7,6},{8,9},{9,8},{10,11... | collective-permute-start | bytes 12296 | tf_op jit(solution)/shard_map/ppermute | solution.py:110
  35.4 0.8 %collective-permute-done.1 = f32[8,128]{1,0:T(8,128)S(1)} collective-permute-done((f32[8,128]{1,0:T(8,128)S(1)}, f32[8,128]{1,0:T(8,128)S(1)}, u32[]{:S(2)}, u32[]{:S(2)}) %collective-permute-start.1) | collective-permute-done | bytes 4128 | tf_op jit(solution)/shard_map/ppermute | solution.py:110
  36.2 0.6 multiply_bitcast_fusion
  36.8 7.0 %shard_map.42 = bf16[4,528,256]{2,1,0:T(8,128)(2,1)} custom-call(f32[512,2048]{1,0:T(8,128)} %get-tuple-element.4.z_ref, f32[16,128]{1,0:T(8,128)} %get-tuple-element.7.tot_ref, bf16[2048,1024]{1,0:T(8,128)(2,1)} %emb_ref.3), custom_call_target="tpu_custom_call" | custom-call | tf_op jit(solution)/shard_map/pallas_call | solution.py:117
  43.8 4.0 %all-to-all-start.1 = ((bf16[4,528,256]{2,1,0:T(8,128)(2,1)}), bf16[4,528,256]{2,1,0:T(8,128)(2,1)S(1)}, u32[]{:S(2)}, u32[]{:S(2)}) async-start(bf16[4,528,256]{2,1,0:T(8,128)(2,1)} %shard_map.42), calls=%async_computation.1 | async-start | bytes 2162688 | tf_op jit(solution)/shard_map/all_to_all | solution.py:123
  47.8 1.7 %constant_dynamic-slice_fusion.prior_ref = bf16[512,256]{1,0:T(8,128)(2,1)} fusion(bf16[512,1024]{1,0:T(8,128)(2,1)} %cent_ref.1, s32[]{:T(128)S(6)} %select_n.22), kind=kLoop, calls=%fused_computation.12 | loop fusion | bytes 524292 | tf_op jit(solution)/shard_map/dynamic_slice | solution.py:124
  49.5 13.2 %all-to-all-done.1.parts_ref = bf16[4,528,256]{2,1,0:T(8,128)(2,1)S(1)} async-done(((bf16[4,528,256]{2,1,0:T(8,128)(2,1)}), bf16[4,528,256]{2,1,0:T(8,128)(2,1)S(1)}, u32[]{:S(2)}, u32[]{:S(2)}) %all-to-all-start.1) | async-done | bytes 1081376 | tf_op jit(solution)/shard_map/all_to_all | solution.py:123
  62.8 0.0 copy-start
  62.8 1.0 %copy-done = bf16[4,528,256]{2,1,0:T(8,128)(2,1)} copy-done((bf16[4,528,256]{2,1,0:T(8,128)(2,1)}, bf16[4,528,256]{2,1,0:T(8,128)(2,1)S(1)}, u32[]{:S(2)}) %copy-start) | copy-done | bytes 1081368
  63.8 2.3 %shard_map.43 = f32[512,256]{1,0:T(8,128)} custom-call(bf16[4,528,256]{2,1,0:T(8,128)(2,1)} %copy-done, bf16[512,256]{1,0:T(8,128)(2,1)} %constant_dynamic-slice_fusion.prior_ref), custom_call_target="tpu_custom_call" | custom-call | tf_op jit(solution)/shard_map/pallas_call | solution.py:125
  (8 shorter events, 0.1 us)
Async XLA Ops:
  10.4 4.1 %collective-permute-start = (f32[8,128]{1,0:T(8,128)S(1)}, f32[8,128]{1,0:T(8,128)S(1)}, u32[]{:S(2)}, u32[]{:S(2)}) collective-permute-start(f32[8,128]{1,0:T(8,128)S(1)} %dynamic-slice_bitcast_fusion), channel_id=1, source_target_pairs={{0,1},{1,0},{2,3},{3,2},{4,5},{5,4},{6,7},{7,6},{8,9},{9,8},{10,11... | collective-permute-start | bytes 12296 | tf_op jit(solution)/shard_map/ppermute | solution.py:105
  33.2 3.0 %collective-permute-start.1 = (f32[8,128]{1,0:T(8,128)S(1)}, f32[8,128]{1,0:T(8,128)S(1)}, u32[]{:S(2)}, u32[]{:S(2)}) collective-permute-start(f32[8,128]{1,0:T(8,128)S(1)} %multiply_add_fusion), channel_id=1, source_target_pairs={{0,1},{1,0},{2,3},{3,2},{4,5},{5,4},{6,7},{7,6},{8,9},{9,8},{10,11... | collective-permute-start | bytes 12296 | tf_op jit(solution)/shard_map/ppermute | solution.py:110
  43.8 18.9 %all-to-all-start.1 = ((bf16[4,528,256]{2,1,0:T(8,128)(2,1)}), bf16[4,528,256]{2,1,0:T(8,128)(2,1)S(1)}, u32[]{:S(2)}, u32[]{:S(2)}) async-start(bf16[4,528,256]{2,1,0:T(8,128)(2,1)} %shard_map.42), calls=%async_computation.1 | async-start | bytes 2162688 | tf_op jit(solution)/shard_map/all_to_all | solution.py:123
  62.8 1.0 %copy-start = (bf16[4,528,256]{2,1,0:T(8,128)(2,1)}, bf16[4,528,256]{2,1,0:T(8,128)(2,1)S(1)}, u32[]{:S(2)}) copy-start(bf16[4,528,256]{2,1,0:T(8,128)(2,1)S(1)} %all-to-all-done.1.parts_ref) | copy-start | bytes 3244036

commit v2 on v1

v2 whole, which is shorter than its diff:
```python
import functools
import math

import jax
import jax.numpy as jnp
from jax import lax
from jax.experimental import pallas as pl
from jax.experimental.pallas import tpu as pltpu
from jax.sharding import Mesh, PartitionSpec as P

SOFTNESS = 0.1
PRIOR = 4.0
LOG2E = math.log2(math.e)
LN2 = math.log(2.0)
ROWS = 256
LOADS = 2
LANES = 128
MASS_ROWS = 16
VMEM_LIMIT = 16 * 1024 * 1024
IN_VMEM = pl.BlockSpec(memory_space=pltpu.VMEM)
IN_HBM = pl.BlockSpec(memory_space=pltpu.HBM)


def in_vmem(x):
    return pltpu.with_memory_space_constraint(x, pltpu.VMEM)


def in_hbm(x):
    return pltpu.with_memory_space_constraint(x, pltpu.HBM)


def logits_kernel(scale, emb_hbm, cent_hbm, z_ref, lse_ref, emb_ref, prior_ref, cent_ref, half_sq, sems):
    rows = emb_ref.shape[0]
    cols = prior_ref.shape[1]
    cent_copy = pltpu.make_async_copy(cent_hbm, cent_ref, sems.at[LOADS])
    cent_copy.start()
    load = rows // LOADS
    copies = []
    for k in range(LOADS):
        part = pl.ds(k * load, load)
        copies.append(pltpu.make_async_copy(emb_hbm.at[part, :], emb_ref.at[part, :], sems.at[k]))
        copies[-1].start()
    cent_copy.wait()
    c = cent_ref[...].astype(jnp.float32)
    half_sq[...] = jnp.broadcast_to(0.5 * jnp.sum(c * c, axis=1, keepdims=True), half_sq.shape)
    first_col = pl.multiple_of(lax.axis_index("x") * cols, cols)
    prior_ref[...] = cent_ref[:, pl.ds(first_col, cols)]
    for r in range(0, rows, ROWS):
        if r % load == 0:
            copies[r // load].wait()
        inner = lax.dot_general(
            cent_ref[...], emb_ref[r : r + ROWS, :], (((1,), (1,)), ((), ())), preferred_element_type=jnp.float32
        )
        z = (inner - half_sq[:, :1]) * scale
        z_ref[:, r : r + ROWS] = z
        top = jnp.max(z, axis=0, keepdims=True)
        lse = top + jnp.log2(jnp.sum(jnp.exp2(z - top), axis=0, keepdims=True))
        for k in range(ROWS // LANES):
            lse_ref[pl.ds(r // LANES + k, 1), :] = lse[:, k * LANES : (k + 1) * LANES]


def merge(lse):
    top = jnp.max(lse, axis=0)
    return top + jnp.log2(jnp.sum(jnp.exp2(lse - top), axis=0))


def weights_kernel(z_ref, every_ref, emb_ref, parts_ref, log_totals_ref, w_ref):
    cents, rows = z_ref.shape
    n_dp, _, cols = parts_ref.shape
    totals = merge(every_ref[...])
    log_totals_ref[...] = totals * LN2
    mass = jnp.zeros((cents, LANES), jnp.float32)
    for k in range(rows // LANES):
        w = jnp.exp2(z_ref[:, k * LANES : (k + 1) * LANES] - totals[k : k + 1, :]).astype(jnp.bfloat16)
        w_ref[:, k * LANES : (k + 1) * LANES] = w
        mass = mass + w.astype(jnp.float32)
    for d in range(n_dp):
        parts_ref[d, :cents, :] = jnp.dot(
            w_ref[...], emb_ref[:, d * cols : (d + 1) * cols], preferred_element_type=jnp.float32
        ).astype(jnp.bfloat16)
    mass = jnp.broadcast_to(jnp.sum(mass, axis=1, keepdims=True), (cents, LANES)).T
    half = MASS_ROWS // 2
    mass = jnp.concatenate([mass[:half, :cols], mass[:half, cols:]], axis=0).astype(jnp.bfloat16)
    for d in range(n_dp):
        parts_ref[d, cents:, :] = mass


def update_kernel(parts_ref, prior_ref, out_ref):
    n_dp = parts_ref.shape[0]
    cents, cols = out_ref.shape
    total = PRIOR * prior_ref[...].astype(jnp.float32)
    mass = jnp.full((MASS_ROWS, cols), PRIOR, jnp.float32)
    for d in range(n_dp):
        total = total + parts_ref[d, :cents, :].astype(jnp.float32)
        mass = mass + parts_ref[d, cents:, :].astype(jnp.float32)
    half = MASS_ROWS // 2
    mass = jnp.concatenate([mass[:1, :], mass[half : half + 1, :]], axis=1)
    inv = 1.0 / jnp.broadcast_to(mass, (LANES, cents)).T
    for k in range(cols // LANES):
        out_ref[:, k * LANES : (k + 1) * LANES] = total[:, k * LANES : (k + 1) * LANES] * inv


def shards(n_dp, emb, cent):
    rows, width = emb.shape
    cents = cent.shape[0]
    cols = width // n_dp
    scale = 2.0 * LOG2E / (SOFTNESS * math.sqrt(width))
    params = pltpu.CompilerParams(vmem_limit_bytes=VMEM_LIMIT)
    z, lse, emb_vmem, prior = pl.pallas_call(
        functools.partial(logits_kernel, scale),
        in_specs=[IN_HBM] * 2,
        out_specs=[IN_VMEM] * 4,
        out_shape=[
            pltpu.VMEM((cents, rows), jnp.float32),
            pltpu.VMEM((rows // LANES, LANES), jnp.float32),
            pltpu.VMEM(emb.shape, emb.dtype),
            pltpu.VMEM((cents, cols), cent.dtype),
        ],
        scratch_shapes=[
            pltpu.VMEM(cent.shape, cent.dtype),
            pltpu.VMEM((cents, LANES), jnp.float32),
            pltpu.SemaphoreType.DMA((LOADS + 1,)),
        ],
        compiler_params=params,
    )(in_hbm(emb), in_hbm(cent))

    other = lax.ppermute(lse, "core", [(0, 1), (1, 0)])
    chip = merge(jnp.stack([lse, other]))
    chips = lax.axis_size("z") * lax.axis_size("y")
    every = lax.all_to_all(jnp.broadcast_to(chip, (chips,) + chip.shape), ("z", "y"), 0, 0)

    parts, log_totals = pl.pallas_call(
        weights_kernel,
        in_specs=[IN_VMEM] * 3,
        out_specs=[IN_VMEM] * 2,
        out_shape=[
            pltpu.VMEM((n_dp, cents + MASS_ROWS, cols), jnp.bfloat16),
            jax.ShapeDtypeStruct(lse.shape, jnp.float32),
        ],
        scratch_shapes=[pltpu.VMEM((cents, rows), jnp.bfloat16)],
        compiler_params=params,
    )(in_vmem(z), in_vmem(every), in_vmem(emb_vmem))
    parts = lax.all_to_all(parts, "x", 0, 0)
    new_centroids = pl.pallas_call(
        update_kernel,
        in_specs=[IN_VMEM] * 2,
        out_specs=IN_VMEM,
        out_shape=jax.ShapeDtypeStruct((cents, cols), jnp.float32),
        compiler_params=params,
    )(in_vmem(parts), in_vmem(prior))
    return new_centroids, log_totals.reshape(rows)


def solution(mesh):
    n_dp = mesh.shape["dp"]
    fine = Mesh(mesh.devices.reshape(n_dp, 8, 4, 2), ("x", "z", "y", "core"))
    cent = ("z", "y", "core")
    return jax.shard_map(
        functools.partial(shards, n_dp),
        mesh=fine,
        in_specs=(P("x", None), P(cent, None)),
        out_specs=(P(cent, "x"), P("x")),
        check_vma=False,
    )
```

time: 66.5 us -> 52.9 us (0.80)
  the two profiles are of different devices: /device:TPU:1 before, /device:TPU:2 now
where the time goes in v2:
time: 52.9 us; the launch traced here: 52.7 us
  blocking collectives  41.5 us (78%)
  Pallas kernels  9.21 us (17%)
  waiting for transfers between devices  1.16 us (2%)
  between operations  0.66 us (1%)
    all_to_all x1, blocking collectives, shards(): lax.all_to_all(jnp.broadcast_to(chip, (chips,) + chip.shape), ('z', 'y'),...  24.5 us
    all_to_all x1, blocking collectives, shards(): parts = lax.all_to_all(parts, 'x', 0, 0)  17 us
    pallas_call x1, Pallas kernels, shards(): pl.pallas_call(functools.partial(logits_kernel, scale), in_specs=[IN_HBM]...  5.13 us
    pallas_call x1, Pallas kernels, shards(): pl.pallas_call(weights_kernel, in_specs=[IN_VMEM] * 3, out_specs=[IN_VMEM...  3.08 us
    ppermute x1, waiting for transfers between devices, shards(): other = lax.ppermute(lse, 'core', [(0, 1), (1, 0)])  1.16 us
  transfers between devices with their start and end apart: 1, of which 1 were waited for; matrix products, arithmetic and copies ran while one was open for 0% of the time, Pallas kernels for 0%

profile of v2, /device:TPU:2, one launch (start us, length us, event | category | flops | bytes accessed | tf_op | source)
XLA Modules:
  0.0 52.7 jit_solution(10076345753589176172)
XLA Ops:
  0.6 5.1 %shard_map.41 = (f32[512,2048]{1,0:T(8,128)S(1)}, f32[16,128]{1,0:T(8,128)S(1)}, bf16[2048,1024]{1,0:T(8,128)(2,1)S(1)}, bf16[512,256]{1,0:T(8,128)(2,1)S(1)}) custom-call(bf16[2048,1024]{1,0:T(8,128)(2,1)} %emb_hbm.1, bf16[512,1024]{1,0:T(8,128)(2,1)} %cent_hbm.1), custom_call_target="tpu_custom_call" | custom-call | tf_op jit(solution)/shard_map/pallas_call | solution.py:109
  5.8 0.1 collective-permute-start
  5.9 1.2 %collective-permute-done = f32[16,128]{1,0:T(8,128)S(1)} collective-permute-done((f32[16,128]{1,0:T(8,128)S(1)}, f32[16,128]{1,0:T(8,128)S(1)}, u32[]{:S(2)}, u32[]{:S(2)}) %collective-permute-start) | collective-permute-done | bytes 8224 | tf_op jit(solution)/shard_map/ppermute | solution.py:127
  7.1 24.5 %all_to_all.10.every_ref = f32[32,16,128]{2,1,0:T(8,128)S(1)} all-to-all(f32[32,16,128]{2,1,0:T(8,128)S(1)} %broadcast_in_dim.4), channel_id=1, replica_groups=mesh['x'=4,'z'=8,'y'=4,'core'=2] {'z','y'}, dimensions={0} | all-to-all | bytes 524288 | tf_op jit(solution)/shard_map/all_to_all | solution.py:130
  31.6 3.1 %shard_map.42 = (bf16[4,528,256]{2,1,0:T(8,128)(2,1)S(1)}, f32[16,128]{1,0:T(8,128)}) custom-call(f32[512,2048]{1,0:T(8,128)S(1)} %get-tuple-element.8.z_ref, f32[32,16,128]{2,1,0:T(8,128)S(1)} %all_to_all.10.every_ref, bf16[2048,1024]{1,0:T(8,128)(2,1)S(1)} %get-tuple-element.10.emb_ref), custom_call_target="tpu_custom_call" | custom-call | tf_op jit(solution)/shard_map/pallas_call | solution.py:132
  34.7 17.0 %all_to_all.11.parts_ref = bf16[4,528,256]{2,1,0:T(8,128)(2,1)S(1)} all-to-all(bf16[4,528,256]{2,1,0:T(8,128)(2,1)S(1)} %get-tuple-element.11), channel_id=1, replica_groups=mesh['x'=4,'z'=8,'y'=4,'core'=2] {'x'}, dimensions={0} | all-to-all | bytes 2162688 | tf_op jit(solution)/shard_map/all_to_all | solution.py:143
  51.7 1.0 %shard_map.43 = f32[512,256]{1,0:T(8,128)} custom-call(bf16[4,528,256]{2,1,0:T(8,128)(2,1)S(1)} %all_to_all.11.parts_ref, bf16[512,256]{1,0:T(8,128)(2,1)S(1)} %get-tuple-element.12.prior_ref), custom_call_target="tpu_custom_call" | custom-call | tf_op jit(solution)/shard_map/pallas_call | solution.py:144
  (4 shorter events, 0.0 us)
Async XLA Ops:
  5.8 1.3 %collective-permute-start = (f32[16,128]{1,0:T(8,128)S(1)}, f32[16,128]{1,0:T(8,128)S(1)}, u32[]{:S(2)}, u32[]{:S(2)}) collective-permute-start(f32[16,128]{1,0:T(8,128)S(1)} %get-tuple-element.9), channel_id=1, source_target_pairs={{0,1},{1,0},{2,3},{3,2},{4,5},{5,4},{6,7},{7,6},{8,9},{9,8},{10,11... | collective-permute-start | bytes 24584 | tf_op jit(solution)/shard_map/ppermute | solution.py:127

commit v3 on v2

--- a/solution.py
+++ b/solution.py
@@ -64,9 +64,12 @@
     return top + jnp.log2(jnp.sum(jnp.exp2(lse - top), axis=0))
 
 
-def weights_kernel(z_ref, every_ref, emb_ref, parts_ref, log_totals_ref, w_ref):
+def weights_kernel(shifts, z_ref, every_ref, emb_ref, *refs):
+    parts_refs = refs[: len(shifts)]
+    w_ref, mass_ref, log_totals_ref = refs[len(shifts) :]
     cents, rows = z_ref.shape
-    n_dp, _, cols = parts_ref.shape
+    cols = mass_ref.shape[1]
+    n_dp = emb_ref.shape[1] // cols
     totals = merge(every_ref[...])
     log_totals_ref[...] = totals * LN2
     mass = jnp.zeros((cents, LANES), jnp.float32)
@@ -74,25 +77,35 @@
         w = jnp.exp2(z_ref[:, k * LANES : (k + 1) * LANES] - totals[k : k + 1, :]).astype(jnp.bfloat16)
         w_ref[:, k * LANES : (k + 1) * LANES] = w
         mass = mass + w.astype(jnp.float32)
-    for d in range(n_dp):
-        parts_ref[d, :cents, :] = jnp.dot(
-            w_ref[...], emb_ref[:, d * cols : (d + 1) * cols], preferred_element_type=jnp.float32
+    me = lax.axis_index("x")
+    for shift, parts_ref in zip(shifts, parts_refs):
+        first_col = pl.multiple_of(lax.rem(me + shift, n_dp) * cols, cols)
+        parts_ref[:cents, :] = jnp.dot(
+            w_ref[...], emb_ref[:, pl.ds(first_col, cols)], preferred_element_type=jnp.float32
         ).astype(jnp.bfloat16)
     mass = jnp.broadcast_to(jnp.sum(mass, axis=1, keepdims=True), (cents, LANES)).T
     half = MASS_ROWS // 2
     mass = jnp.concatenate([mass[:half, :cols], mass[:half, cols:]], axis=0).astype(jnp.bfloat16)
-    for d in range(n_dp):
-        parts_ref[d, cents:, :] = mass
+    mass_ref[...] = mass
+    for parts_ref in parts_refs:
+        parts_ref[cents:, :] = mass
 
 
-def update_kernel(parts_ref, prior_ref, out_ref):
-    n_dp = parts_ref.shape[0]
+def own_kernel(w_ref, emb_ref, prior_ref, out_ref):
+    cols = out_ref.shape[1]
+    first_col = pl.multiple_of(lax.axis_index("x") * cols, cols)
+    own = jnp.dot(w_ref[...], emb_ref[:, pl.ds(first_col, cols)], preferred_element_type=jnp.float32)
+    out_ref[...] = own + PRIOR * prior_ref[...].astype(jnp.float32)
+
+
+def update_kernel(own_ref, mass_ref, *refs):
+    parts_refs, out_ref = refs[:-1], refs[-1]
     cents, cols = out_ref.shape
-    total = PRIOR * prior_ref[...].astype(jnp.float32)
-    mass = jnp.full((MASS_ROWS, cols), PRIOR, jnp.float32)
-    for d in range(n_dp):
-        total = total + parts_ref[d, :cents, :].astype(jnp.float32)
-        mass = mass + parts_ref[d, cents:, :].astype(jnp.float32)
+    total = own_ref[...]
+    mass = PRIOR + mass_ref[...].astype(jnp.float32)
+    for parts_ref in parts_refs:
+        total = total + parts_ref[:cents, :].astype(jnp.float32)
+        mass = mass + parts_ref[cents:, :].astype(jnp.float32)
     half = MASS_ROWS // 2
     mass = jnp.concatenate([mass[:1, :], mass[half : half + 1, :]], axis=1)
     inv = 1.0 / jnp.broadcast_to(mass, (LANES, cents)).T
@@ -129,25 +142,37 @@
     chips = lax.axis_size("z") * lax.axis_size("y")
     every = lax.all_to_all(jnp.broadcast_to(chip, (chips,) + chip.shape), ("z", "y"), 0, 0)
 
-    parts, log_totals = pl.pallas_call(
-        weights_kernel,
+    shifts = [n_dp // 2] + [k for k in range(1, n_dp) if k != n_dp // 2]
+    part = pltpu.VMEM((cents + MASS_ROWS, cols), jnp.bfloat16)
+    *parts, w, mass, log_totals = pl.pallas_call(
+        functools.partial(weights_kernel, shifts),
         in_specs=[IN_VMEM] * 3,
-        out_specs=[IN_VMEM] * 2,
-        out_shape=[
-            pltpu.VMEM((n_dp, cents + MASS_ROWS, cols), jnp.bfloat16),
+        out_specs=[IN_VMEM] * (len(shifts) + 3),
+        out_shape=[part] * len(shifts)
+        + [
+            pltpu.VMEM((cents, rows), jnp.bfloat16),
+            pltpu.VMEM((MASS_ROWS, cols), jnp.bfloat16),
             jax.ShapeDtypeStruct(lse.shape, jnp.float32),
         ],
-        scratch_shapes=[pltpu.VMEM((cents, rows), jnp.bfloat16)],
         compiler_params=params,
     )(in_vmem(z), in_vmem(every), in_vmem(emb_vmem))
-    parts = lax.all_to_all(parts, "x", 0, 0)
+    parts = [
+        lax.ppermute(p, "x", [(k, (k + shift) % n_dp) for k in range(n_dp)]) for shift, p in zip(shifts, parts)
+    ]
+    own = pl.pallas_call(
+        own_kernel,
+        in_specs=[IN_VMEM] * 3,
+        out_specs=IN_VMEM,
+        out_shape=pltpu.VMEM((cents, cols), jnp.float32),
+        compiler_params=params,
+    )(in_vmem(w), in_vmem(emb_vmem), in_vmem(prior))
     new_centroids = pl.pallas_call(
         update_kernel,
-        in_specs=[IN_VMEM] * 2,
+        in_specs=[IN_VMEM] * (2 + len(parts)),
         out_specs=IN_VMEM,
         out_shape=jax.ShapeDtypeStruct((cents, cols), jnp.float32),
         compiler_params=params,
-    )(in_vmem(parts), in_vmem(prior))
+    )(in_vmem(own), in_vmem(mass), *[in_vmem(p) for p in parts])
     return new_centroids, log_totals.reshape(rows)
 
 

time: 52.9 us -> 49.5 us (0.936)
  the two profiles are of different devices: /device:TPU:2 before, /device:TPU:3 now
where the time goes in v3:
time: 49.5 us; the launch traced here: 49.4 us
  blocking collectives  22.6 us (46%)
  waiting for transfers between devices  12.3 us (25%)
  Pallas kernels  9.62 us (19%)
  starting transfers between devices  4.09 us (8%)
  between operations  0.66 us (1%)
    all_to_all x1, blocking collectives, shards(): lax.all_to_all(jnp.broadcast_to(chip, (chips,) + chip.shape), ('z', 'y'),...  22.6 us
    ppermute x3, waiting for transfers between devices, shards(): lax.ppermute(p, 'x', [(k, (k + shift) % n_dp) for k in range(n_dp)])  11.5 us
    pallas_call x1, Pallas kernels, shards(): pl.pallas_call(functools.partial(logits_kernel, scale), in_specs=[IN_HBM]...  5.13 us
    ppermute x3, starting transfers between devices, shards(): lax.ppermute(p, 'x', [(k, (k + shift) % n_dp) for k in range(n_dp)])  3.33 us
    pallas_call x1, Pallas kernels, shards(): pl.pallas_call(functools.partial(weights_kernel, shifts), in_specs=[IN_VM...  2.8 us
  transfers between devices with their start and end apart: 4, of which 4 were waited for; matrix products, arithmetic and copies ran while one was open for 0% of the time, Pallas kernels for 2%

profile of v3, /device:TPU:3, one launch (start us, length us, event | category | flops | bytes accessed | tf_op | source)
XLA Modules:
  0.0 49.4 jit_solution(7206295974888864096)
XLA Ops:
  0.6 5.1 %shard_map.41 = (f32[512,2048]{1,0:T(8,128)S(1)}, f32[16,128]{1,0:T(8,128)S(1)}, bf16[2048,1024]{1,0:T(8,128)(2,1)S(1)}, bf16[512,256]{1,0:T(8,128)(2,1)S(1)}) custom-call(bf16[2048,1024]{1,0:T(8,128)(2,1)} %emb_hbm.1, bf16[512,1024]{1,0:T(8,128)(2,1)} %cent_hbm.1), custom_call_target="tpu_custom_call" | custom-call | tf_op jit(solution)/shard_map/pallas_call | solution.py:122
  5.8 0.8 %collective-permute-start = (f32[16,128]{1,0:T(8,128)S(1)}, f32[16,128]{1,0:T(8,128)S(1)}, u32[]{:S(2)}, u32[]{:S(2)}) collective-permute-start(f32[16,128]{1,0:T(8,128)S(1)} %get-tuple-element.13), channel_id=1, source_target_pairs={{0,1},{1,0},{2,3},{3,2},{4,5},{5,4},{6,7},{7,6},{8,9},{9,8},{10,11... | collective-permute-start | bytes 24584 | tf_op jit(solution)/shard_map/ppermute | solution.py:140
  6.5 0.8 %collective-permute-done = f32[16,128]{1,0:T(8,128)S(1)} collective-permute-done((f32[16,128]{1,0:T(8,128)S(1)}, f32[16,128]{1,0:T(8,128)S(1)}, u32[]{:S(2)}, u32[]{:S(2)}) %collective-permute-start) | collective-permute-done | bytes 8224 | tf_op jit(solution)/shard_map/ppermute | solution.py:140
  7.4 22.6 %all_to_all.5.every_ref = f32[32,16,128]{2,1,0:T(8,128)S(1)} all-to-all(f32[32,16,128]{2,1,0:T(8,128)S(1)} %broadcast_in_dim.4), channel_id=1, replica_groups=mesh['x'=4,'z'=8,'y'=4,'core'=2] {'z','y'}, dimensions={0} | all-to-all | bytes 524288 | tf_op jit(solution)/shard_map/all_to_all | solution.py:143
  30.0 2.8 %shard_map.42 = (bf16[528,256]{1,0:T(8,128)(2,1)S(1)}, bf16[528,256]{1,0:T(8,128)(2,1)S(1)}, bf16[528,256]{1,0:T(8,128)(2,1)S(1)}, bf16[512,2048]{1,0:T(8,128)(2...) custom-call(f32[512,2048]{1,0:T(8,128)S(1)} %get-tuple-element.12.z_ref, ...), custom_call_target="tpu_custom_call" | custom-call | tf_op jit(solution)/shard_map/pallas_call | solution.py:147
  32.8 1.9 %collective-permute-start.1 = (bf16[528,256]{1,0:T(8,128)(2,1)S(1)}, bf16[528,256]{1,0:T(8,128)(2,1)S(1)}, u32[]{:S(2)}, u32[]{:S(2)}) collective-permute-start(bf16[528,256]{1,0:T(8,128)(2,1)S(1)} %get-tuple-element.18), channel_id=1, source_target_pairs={{0,128},{64,192},{128,0},{192,64},{1,129},{65,193},{129,1},{193,65... | collective-permute-start | bytes 811016 | tf_op jit(solution)/shard_map/ppermute | solution.py:160
  34.7 0.0 collective-permute-start.2
  34.7 1.5 %collective-permute-start.3 = (bf16[528,256]{1,0:T(8,128)(2,1)S(1)}, bf16[528,256]{1,0:T(8,128)(2,1)S(1)}, u32[]{:S(2)}, u32[]{:S(2)}) collective-permute-start(bf16[528,256]{1,0:T(8,128)(2,1)S(1)} %get-tuple-element.20), channel_id=1, source_target_pairs={{0,192},{64,0},{128,64},{192,128},{1,193},{65,1},{129,65},{193,129... | collective-permute-start | bytes 811016 | tf_op jit(solution)/shard_map/ppermute | solution.py:160
  36.2 0.7 %shard_map.43.own_ref = f32[512,256]{1,0:T(8,128)S(1)} custom-call(bf16[512,2048]{1,0:T(8,128)(2,1)S(1)} %get-tuple-element.15.w_ref, bf16[2048,1024]{1,0:T(8,128)(2,1)S(1)} %get-tuple-element.14.emb_ref, bf16[512,256]{1,0:T(8,128)(2,1)S(1)} %get-tuple-element.16.prior_ref), custom_call_target="tpu_custom_call" | custom-call | tf_op jit(solution)/shard_map/pallas_call | solution.py:162
  36.9 3.2 %collective-permute-done.1.refs_0_ = bf16[528,256]{1,0:T(8,128)(2,1)S(1)} collective-permute-done((bf16[528,256]{1,0:T(8,128)(2,1)S(1)}, bf16[528,256]{1,0:T(8,128)(2,1)S(1)}, u32[]{:S(2)}, u32[]{:S(2)}) %collective-permute-start.1) | collective-permute-done | bytes 270368 | tf_op jit(solution)/shard_map/ppermute | solution.py:160
  40.1 5.8 %collective-permute-done.2.refs_1_ = bf16[528,256]{1,0:T(8,128)(2,1)S(1)} collective-permute-done((bf16[528,256]{1,0:T(8,128)(2,1)S(1)}, bf16[528,256]{1,0:T(8,128)(2,1)S(1)}, u32[]{:S(2)}, u32[]{:S(2)}) %collective-permute-start.2) | collective-permute-done | bytes 270368 | tf_op jit(solution)/shard_map/ppermute | solution.py:160
  45.9 2.5 %collective-permute-done.3.refs_2_ = bf16[528,256]{1,0:T(8,128)(2,1)S(1)} collective-permute-done((bf16[528,256]{1,0:T(8,128)(2,1)S(1)}, bf16[528,256]{1,0:T(8,128)(2,1)S(1)}, u32[]{:S(2)}, u32[]{:S(2)}) %collective-permute-start.3) | collective-permute-done | bytes 270368 | tf_op jit(solution)/shard_map/ppermute | solution.py:160
  48.4 1.0 %shard_map.44 = f32[512,256]{1,0:T(8,128)} custom-call(f32[512,256]{1,0:T(8,128)S(1)} %shard_map.43.own_ref, bf16[16,256]{1,0:T(8,128)(2,1)S(1)} %get-tuple-element.17.mass_ref, bf16[528,256]{1,0:T(8,128)(2,1)S(1)} %collective-permute-done.1.refs_0_, bf16[528,256]{1,0:T(8,128)(2,1)S(1)} %collective-permute-done.2.refs_1_, ...), custom_call_target="tpu_custom_call" | custom-call | tf_op jit(solution)/shard_map/pallas_call | solution.py:169
  (4 shorter events, 0.0 us)
Async XLA Ops:
  5.8 1.6 %collective-permute-start = (f32[16,128]{1,0:T(8,128)S(1)}, f32[16,128]{1,0:T(8,128)S(1)}, u32[]{:S(2)}, u32[]{:S(2)}) collective-permute-start(f32[16,128]{1,0:T(8,128)S(1)} %get-tuple-element.13), channel_id=1, source_target_pairs={{0,1},{1,0},{2,3},{3,2},{4,5},{5,4},{6,7},{7,6},{8,9},{9,8},{10,11... | collective-permute-start | bytes 24584 | tf_op jit(solution)/shard_map/ppermute | solution.py:140
  32.8 7.3 %collective-permute-start.1 = (bf16[528,256]{1,0:T(8,128)(2,1)S(1)}, bf16[528,256]{1,0:T(8,128)(2,1)S(1)}, u32[]{:S(2)}, u32[]{:S(2)}) collective-permute-start(bf16[528,256]{1,0:T(8,128)(2,1)S(1)} %get-tuple-element.18), channel_id=1, source_target_pairs={{0,128},{64,192},{128,0},{192,64},{1,129},{65,193},{129,1},{193,65... | collective-permute-start | bytes 811016 | tf_op jit(solution)/shard_map/ppermute | solution.py:160
  34.7 11.2 %collective-permute-start.2 = (bf16[528,256]{1,0:T(8,128)(2,1)S(1)}, bf16[528,256]{1,0:T(8,128)(2,1)S(1)}, u32[]{:S(2)}, u32[]{:S(2)}) collective-permute-start(bf16[528,256]{1,0:T(8,128)(2,1)S(1)} %get-tuple-element.19), channel_id=1, source_target_pairs={{0,64},{64,128},{128,192},{192,0},{1,65},{65,129},{129,193},{193,1... | collective-permute-start | bytes 811016 | tf_op jit(solution)/shard_map/ppermute | solution.py:160
  34.7 13.7 %collective-permute-start.3 = (bf16[528,256]{1,0:T(8,128)(2,1)S(1)}, bf16[528,256]{1,0:T(8,128)(2,1)S(1)}, u32[]{:S(2)}, u32[]{:S(2)}) collective-permute-start(bf16[528,256]{1,0:T(8,128)(2,1)S(1)} %get-tuple-element.20), channel_id=1, source_target_pairs={{0,192},{64,0},{128,64},{192,128},{1,193},{65,1},{129,65},{193,129... | collective-permute-start | bytes 811016 | tf_op jit(solution)/shard_map/ppermute | solution.py:160

commit v4 on v2

--- a/solution.py
+++ b/solution.py
@@ -64,9 +64,8 @@
     return top + jnp.log2(jnp.sum(jnp.exp2(lse - top), axis=0))
 
 
-def weights_kernel(z_ref, every_ref, emb_ref, parts_ref, log_totals_ref, w_ref):
+def weights_kernel(shift, z_ref, every_ref, emb_ref, part_ref, w_ref, mass_ref, log_totals_ref):
     cents, rows = z_ref.shape
-    n_dp, _, cols = parts_ref.shape
     totals = merge(every_ref[...])
     log_totals_ref[...] = totals * LN2
     mass = jnp.zeros((cents, LANES), jnp.float32)
@@ -74,28 +73,48 @@
         w = jnp.exp2(z_ref[:, k * LANES : (k + 1) * LANES] - totals[k : k + 1, :]).astype(jnp.bfloat16)
         w_ref[:, k * LANES : (k + 1) * LANES] = w
         mass = mass + w.astype(jnp.float32)
-    for d in range(n_dp):
-        parts_ref[d, :cents, :] = jnp.dot(
-            w_ref[...], emb_ref[:, d * cols : (d + 1) * cols], preferred_element_type=jnp.float32
-        ).astype(jnp.bfloat16)
+    cols = mass_ref.shape[1]
     mass = jnp.broadcast_to(jnp.sum(mass, axis=1, keepdims=True), (cents, LANES)).T
     half = MASS_ROWS // 2
-    mass = jnp.concatenate([mass[:half, :cols], mass[:half, cols:]], axis=0).astype(jnp.bfloat16)
-    for d in range(n_dp):
-        parts_ref[d, cents:, :] = mass
-
-
-def update_kernel(parts_ref, prior_ref, out_ref):
-    n_dp = parts_ref.shape[0]
+    mass_ref[...] = jnp.concatenate([mass[:half, :cols], mass[:half, cols:]], axis=0).astype(jnp.bfloat16)
+    part_product(shift, w_ref, emb_ref, mass_ref, part_ref)
+
+
+def part_product(shift, w_ref, emb_ref, mass_ref, part_ref):
+    cents = w_ref.shape[0]
+    cols = mass_ref.shape[1]
+    n_dp = emb_ref.shape[1] // cols
+    first_col = pl.multiple_of(lax.rem(lax.axis_index("x") + shift, n_dp) * cols, cols)
+    part_ref[:cents, :] = jnp.dot(
+        w_ref[...], emb_ref[:, pl.ds(first_col, cols)], preferred_element_type=jnp.float32
+    ).astype(jnp.bfloat16)
+    part_ref[cents:, :] = mass_ref[...]
+
+
+def parts_kernel(shifts, w_ref, emb_ref, mass_ref, *parts_refs):
+    for shift, part_ref in zip(shifts, parts_refs):
+        part_product(shift, w_ref, emb_ref, mass_ref, part_ref)
+
+
+def own_kernel(w_ref, emb_ref, prior_ref, mass_ref, far_ref, out_ref, out_mass_ref):
     cents, cols = out_ref.shape
-    total = PRIOR * prior_ref[...].astype(jnp.float32)
-    mass = jnp.full((MASS_ROWS, cols), PRIOR, jnp.float32)
-    for d in range(n_dp):
-        total = total + parts_ref[d, :cents, :].astype(jnp.float32)
-        mass = mass + parts_ref[d, cents:, :].astype(jnp.float32)
+    first_col = pl.multiple_of(lax.axis_index("x") * cols, cols)
+    own = jnp.dot(w_ref[...], emb_ref[:, pl.ds(first_col, cols)], preferred_element_type=jnp.float32)
+    out_ref[...] = own + PRIOR * prior_ref[...].astype(jnp.float32) + far_ref[:cents, :].astype(jnp.float32)
+    out_mass_ref[...] = PRIOR + mass_ref[...].astype(jnp.float32) + far_ref[cents:, :].astype(jnp.float32)
+
+
+def update_kernel(own_ref, mass_ref, *refs):
+    parts_refs, out_ref = refs[:-1], refs[-1]
+    cents, cols = out_ref.shape
+    total = own_ref[...]
+    mass = mass_ref[...]
+    for part_ref in parts_refs:
+        total = total + part_ref[:cents, :].astype(jnp.float32)
+        mass = mass + part_ref[cents:, :].astype(jnp.float32)
     half = MASS_ROWS // 2
-    mass = jnp.concatenate([mass[:1, :], mass[half : half + 1, :]], axis=1)
-    inv = 1.0 / jnp.broadcast_to(mass, (LANES, cents)).T
+    inv = 1.0 / jnp.concatenate([mass[:1, :], mass[half : half + 1, :]], axis=1)
+    inv = jnp.broadcast_to(inv, (LANES, cents)).T
     for k in range(cols // LANES):
         out_ref[:, k * LANES : (k + 1) * LANES] = total[:, k * LANES : (k + 1) * LANES] * inv
 
@@ -127,27 +146,49 @@
     other = lax.ppermute(lse, "core", [(0, 1), (1, 0)])
     chip = merge(jnp.stack([lse, other]))
     chips = lax.axis_size("z") * lax.axis_size("y")
-    every = lax.all_to_all(jnp.broadcast_to(chip, (chips,) + chip.shape), ("z", "y"), 0, 0)
-
-    parts, log_totals = pl.pallas_call(
-        weights_kernel,
+    every = lax.all_to_all(jnp.broadcast_to(chip, (chips,) + chip.shape), ("y", "z"), 0, 0)
+
+    part = pltpu.VMEM((cents + MASS_ROWS, cols), jnp.bfloat16)
+    first = n_dp // 2
+    others = [k for k in range(1, n_dp) if k != first]
+    far, w, mass, log_totals = pl.pallas_call(
+        functools.partial(weights_kernel, first),
         in_specs=[IN_VMEM] * 3,
-        out_specs=[IN_VMEM] * 2,
+        out_specs=[IN_VMEM] * 4,
         out_shape=[
-            pltpu.VMEM((n_dp, cents + MASS_ROWS, cols), jnp.bfloat16),
+            part,
+            pltpu.VMEM((cents, rows), jnp.bfloat16),
+            pltpu.VMEM((MASS_ROWS, cols), jnp.bfloat16),
             jax.ShapeDtypeStruct(lse.shape, jnp.float32),
         ],
-        scratch_shapes=[pltpu.VMEM((cents, rows), jnp.bfloat16)],
         compiler_params=params,
     )(in_vmem(z), in_vmem(every), in_vmem(emb_vmem))
-    parts = lax.all_to_all(parts, "x", 0, 0)
+
+    def send(p, shift):
+        return lax.ppermute(p, "x", [(k, (k + shift) % n_dp) for k in range(n_dp)])
+
+    near = pl.pallas_call(
+        functools.partial(parts_kernel, others),
+        in_specs=[IN_VMEM] * 3,
+        out_specs=[IN_VMEM] * len(others),
+        out_shape=[part] * len(others),
+        compiler_params=params,
+    )(in_vmem(w), in_vmem(emb_vmem), in_vmem(mass))
+    own, own_mass = pl.pallas_call(
+        own_kernel,
+        in_specs=[IN_VMEM] * 5,
+        out_specs=[IN_VMEM] * 2,
+        out_shape=[pltpu.VMEM((cents, cols), jnp.float32), pltpu.VMEM((MASS_ROWS, cols), jnp.float32)],
+        compiler_params=params,
+    )(in_vmem(w), in_vmem(emb_vmem), in_vmem(prior), in_vmem(mass), in_vmem(send(far, first)))
+    parts = [send(p, k) for k, p in zip(others, near)]
     new_centroids = pl.pallas_call(
         update_kernel,
-        in_specs=[IN_VMEM] * 2,
+        in_specs=[IN_VMEM] * (2 + len(parts)),
         out_specs=IN_VMEM,
         out_shape=jax.ShapeDtypeStruct((cents, cols), jnp.float32),
         compiler_params=params,
-    )(in_vmem(parts), in_vmem(prior))
+    )(in_vmem(own), in_vmem(own_mass), *[in_vmem(p) for p in parts])
     return new_centroids, log_totals.reshape(rows)
 
 

time: 52.9 us -> 48.6 us (0.919)
  the two profiles are of different devices: /device:TPU:2 before, /device:TPU:38 now
where the time goes in v4:
time: 48.6 us; the launch traced here: 48.5 us
  blocking collectives  23.8 us (49%)
  waiting for transfers between devices  10.3 us (21%)
  Pallas kernels  10 us (21%)
  starting transfers between devices  3.65 us (8%)
  between operations  0.68 us (1%)
    all_to_all x1, blocking collectives, shards(): lax.all_to_all(jnp.broadcast_to(chip, (chips,) + chip.shape), ('y', 'z'),...  23.8 us
    ppermute x3, waiting for transfers between devices, send(): return lax.ppermute(p, 'x', [(k, (k + shift) % n_dp) for k in range(n_dp)])  9.13 us
    pallas_call x1, Pallas kernels, shards(): pl.pallas_call(functools.partial(logits_kernel, scale), in_specs=[IN_HBM]...  5.13 us
    ppermute x3, starting transfers between devices, send(): return lax.ppermute(p, 'x', [(k, (k + shift) % n_dp) for k in range(n_dp)])  3.56 us
    pallas_call x1, Pallas kernels, shards(): pl.pallas_call(functools.partial(weights_kernel, first), in_specs=[IN_VME...  1.92 us
    pallas_call x1, Pallas kernels, shards(): pl.pallas_call(functools.partial(parts_kernel, others), in_specs=[IN_VMEM...  1.27 us
    ppermute x1, waiting for transfers between devices, shards(): other = lax.ppermute(lse, 'core', [(0, 1), (1, 0)])  1.16 us
  transfers between devices with their start and end apart: 4, of which 4 were waited for; matrix products, arithmetic and copies ran while one was open for 0% of the time, Pallas kernels for 4%

profile of v4, /device:TPU:38, one launch (start us, length us, event | category | flops | bytes accessed | tf_op | source)
XLA Modules:
  0.0 48.5 jit_solution(10581453727785497261)
XLA Ops:
  0.6 5.1 %shard_map.41 = (f32[512,2048]{1,0:T(8,128)S(1)}, f32[16,128]{1,0:T(8,128)S(1)}, bf16[2048,1024]{1,0:T(8,128)(2,1)S(1)}, bf16[512,256]{1,0:T(8,128)(2,1)S(1)}) custom-call(bf16[2048,1024]{1,0:T(8,128)(2,1)} %emb_hbm.1, bf16[512,1024]{1,0:T(8,128)(2,1)} %cent_hbm.1), custom_call_target="tpu_custom_call" | custom-call | tf_op jit(solution)/shard_map/pallas_call | solution.py:128
  5.8 0.1 collective-permute-start
  5.9 1.2 %collective-permute-done = f32[16,128]{1,0:T(8,128)S(1)} collective-permute-done((f32[16,128]{1,0:T(8,128)S(1)}, f32[16,128]{1,0:T(8,128)S(1)}, u32[]{:S(2)}, u32[]{:S(2)}) %collective-permute-start) | collective-permute-done | bytes 8224 | tf_op jit(solution)/shard_map/ppermute | solution.py:146
  7.1 23.8 %all_to_all.5.every_ref = f32[32,16,128]{2,1,0:T(8,128)S(1)} all-to-all(f32[32,16,128]{2,1,0:T(8,128)S(1)} %broadcast_in_dim.4), channel_id=1, replica_groups=mesh['x'=4,'z'=8,'y'=4,'core'=2] {'y','z'}, dimensions={0} | all-to-all | bytes 524288 | tf_op jit(solution)/shard_map/all_to_all | solution.py:149
  30.9 1.9 %shard_map.42 = (bf16[528,256]{1,0:T(8,128)(2,1)S(1)}, bf16[512,2048]{1,0:T(8,128)(2,1)S(1)}, bf16[16,256]{1,0:T(8,128)(2,1)S(1)}, f32[16,128]{1,0:T(8,128)}) custom-call(f32[512,2048]{1,0:T(8,128)S(1)} %get-tuple-element.14.z_ref, f32[32,16,128]{2,1,0:T(8,128)S(1)} %all_to_all.5.every_ref, bf16[2048,1024]{1,0:T(8,128)(2,1)S(1)} %get-tuple-element.16.emb_ref), custom_call_target="tpu_custom_call" | custom-call | tf_op jit(solution)/shard_map/pallas_call | solution.py:154
  32.8 1.4 %collective-permute-start.1 = (bf16[528,256]{1,0:T(8,128)(2,1)S(1)}, bf16[528,256]{1,0:T(8,128)(2,1)S(1)}, u32[]{:S(2)}, u32[]{:S(2)}) collective-permute-start(bf16[528,256]{1,0:T(8,128)(2,1)S(1)} %get-tuple-element.20), channel_id=1, source_target_pairs={{0,128},{64,192},{128,0},{192,64},{1,129},{65,193},{129,1},{193,65... | collective-permute-start | bytes 811016 | tf_op jit(solution)/shard_map/ppermute | solution.py:168
  34.2 1.3 %shard_map.44 = (bf16[528,256]{1,0:T(8,128)(2,1)S(1)}, bf16[528,256]{1,0:T(8,128)(2,1)S(1)}) custom-call(bf16[512,2048]{1,0:T(8,128)(2,1)S(1)} %get-tuple-element.17.w_ref, bf16[2048,1024]{1,0:T(8,128)(2,1)S(1)} %get-tuple-element.16.emb_ref, bf16[16,256]{1,0:T(8,128)(2,1)S(1)} %get-tuple-element.19.mass_ref), custom_call_target="tpu_custom_call" | custom-call | tf_op jit(solution)/shard_map/pallas_call | solution.py:170
  35.5 2.2 %collective-permute-start.2 = (bf16[528,256]{1,0:T(8,128)(2,1)S(1)}, bf16[528,256]{1,0:T(8,128)(2,1)S(1)}, u32[]{:S(2)}, u32[]{:S(2)}) collective-permute-start(bf16[528,256]{1,0:T(8,128)(2,1)S(1)} %get-tuple-element.23), channel_id=1, source_target_pairs={{0,64},{64,128},{128,192},{192,0},{1,65},{65,129},{129,193},{193,1... | collective-permute-start | bytes 811016 | tf_op jit(solution)/shard_map/ppermute | solution.py:168
  37.6 0.0 collective-permute-start.3
  37.6 6.1 %collective-permute-done.1.far_ref = bf16[528,256]{1,0:T(8,128)(2,1)S(1)} collective-permute-done((bf16[528,256]{1,0:T(8,128)(2,1)S(1)}, bf16[528,256]{1,0:T(8,128)(2,1)S(1)}, u32[]{:S(2)}, u32[]{:S(2)}) %collective-permute-start.1) | collective-permute-done | bytes 270368 | tf_op jit(solution)/shard_map/ppermute | solution.py:168
  43.7 0.7 %shard_map.43 = (f32[512,256]{1,0:T(8,128)S(1)}, f32[16,256]{1,0:T(8,128)S(1)}) custom-call(bf16[512,2048]{1,0:T(8,128)(2,1)S(1)} %get-tuple-element.17.w_ref, bf16[2048,1024]{1,0:T(8,128)(2,1)S(1)} %get-tuple-element.16.emb_ref, bf16[512,256]{1,0:T(8,128)(2,1)S(1)} %get-tuple-element.18.prior_ref, bf16[16,256]{1,0:T(8,128)(2,1)S(1)} %get-tuple-element.19.mass_ref, ...), custom_call_target="tpu_custom_call" | custom-call | tf_op jit(solution)/shard_map/pallas_call | solution.py:177
  44.5 0.7 %collective-permute-done.2.refs_0_ = bf16[528,256]{1,0:T(8,128)(2,1)S(1)} collective-permute-done((bf16[528,256]{1,0:T(8,128)(2,1)S(1)}, bf16[528,256]{1,0:T(8,128)(2,1)S(1)}, u32[]{:S(2)}, u32[]{:S(2)}) %collective-permute-start.2) | collective-permute-done | bytes 270368 | tf_op jit(solution)/shard_map/ppermute | solution.py:168
  45.1 2.4 %collective-permute-done.3.refs_1_ = bf16[528,256]{1,0:T(8,128)(2,1)S(1)} collective-permute-done((bf16[528,256]{1,0:T(8,128)(2,1)S(1)}, bf16[528,256]{1,0:T(8,128)(2,1)S(1)}, u32[]{:S(2)}, u32[]{:S(2)}) %collective-permute-start.3) | collective-permute-done | bytes 270368 | tf_op jit(solution)/shard_map/ppermute | solution.py:168
  47.5 0.9 %shard_map.45 = f32[512,256]{1,0:T(8,128)} custom-call(f32[512,256]{1,0:T(8,128)S(1)} %get-tuple-element.21.own_ref, f32[16,256]{1,0:T(8,128)S(1)} %get-tuple-element.22.mass_ref, bf16[528,256]{1,0:T(8,128)(2,1)S(1)} %collective-permute-done.2.refs_0_, bf16[528,256]{1,0:T(8,128)(2,1)S(1)} %collective-permute-done.3.refs_1_), custom_call_target="tpu_custom_call" | custom-call | tf_op jit(solution)/shard_map/pallas_call | solution.py:185
  (4 shorter events, 0.0 us)
Async XLA Ops:
  5.8 1.3 %collective-permute-start = (f32[16,128]{1,0:T(8,128)S(1)}, f32[16,128]{1,0:T(8,128)S(1)}, u32[]{:S(2)}, u32[]{:S(2)}) collective-permute-start(f32[16,128]{1,0:T(8,128)S(1)} %get-tuple-element.15), channel_id=1, source_target_pairs={{0,1},{1,0},{2,3},{3,2},{4,5},{5,4},{6,7},{7,6},{8,9},{9,8},{10,11... | collective-permute-start | bytes 24584 | tf_op jit(solution)/shard_map/ppermute | solution.py:146
  32.8 10.9 %collective-permute-start.1 = (bf16[528,256]{1,0:T(8,128)(2,1)S(1)}, bf16[528,256]{1,0:T(8,128)(2,1)S(1)}, u32[]{:S(2)}, u32[]{:S(2)}) collective-permute-start(bf16[528,256]{1,0:T(8,128)(2,1)S(1)} %get-tuple-element.20), channel_id=1, source_target_pairs={{0,128},{64,192},{128,0},{192,64},{1,129},{65,193},{129,1},{193,65... | collective-permute-start | bytes 811016 | tf_op jit(solution)/shard_map/ppermute | solution.py:168
  35.5 9.7 %collective-permute-start.2 = (bf16[528,256]{1,0:T(8,128)(2,1)S(1)}, bf16[528,256]{1,0:T(8,128)(2,1)S(1)}, u32[]{:S(2)}, u32[]{:S(2)}) collective-permute-start(bf16[528,256]{1,0:T(8,128)(2,1)S(1)} %get-tuple-element.23), channel_id=1, source_target_pairs={{0,64},{64,128},{128,192},{192,0},{1,65},{65,129},{129,193},{193,1... | collective-permute-start | bytes 811016 | tf_op jit(solution)/shard_map/ppermute | solution.py:168
  37.6 9.9 %collective-permute-start.3 = (bf16[528,256]{1,0:T(8,128)(2,1)S(1)}, bf16[528,256]{1,0:T(8,128)(2,1)S(1)}, u32[]{:S(2)}, u32[]{:S(2)}) collective-permute-start(bf16[528,256]{1,0:T(8,128)(2,1)S(1)} %get-tuple-element.24), channel_id=1, source_target_pairs={{0,192},{64,0},{128,64},{192,128},{1,193},{65,1},{129,65},{193,129... | collective-permute-start | bytes 811016 | tf_op jit(solution)/shard_map/ppermute | solution.py:168

commit v5 on v4

--- a/solution.py
+++ b/solution.py
@@ -70,9 +70,9 @@
     log_totals_ref[...] = totals * LN2
     mass = jnp.zeros((cents, LANES), jnp.float32)
     for k in range(rows // LANES):
-        w = jnp.exp2(z_ref[:, k * LANES : (k + 1) * LANES] - totals[k : k + 1, :]).astype(jnp.bfloat16)
-        w_ref[:, k * LANES : (k + 1) * LANES] = w
-        mass = mass + w.astype(jnp.float32)
+        w = jnp.exp2(z_ref[:, k * LANES : (k + 1) * LANES] - totals[k : k + 1, :])
+        w_ref[:, k * LANES : (k + 1) * LANES] = w.astype(jnp.bfloat16)
+        mass = mass + w
     cols = mass_ref.shape[1]
     mass = jnp.broadcast_to(jnp.sum(mass, axis=1, keepdims=True), (cents, LANES)).T
     half = MASS_ROWS // 2

time: 48.6 us -> 48.4 us (level)
  no operation moved by 1% of the time
where the time goes in v5:
time: 48.4 us; the launch traced here: 48.3 us
  blocking collectives  23.8 us (49%)
  waiting for transfers between devices  10.3 us (21%)
  Pallas kernels  9.83 us (20%)
  starting transfers between devices  3.65 us (8%)
  between operations  0.68 us (1%)
    all_to_all x1, blocking collectives, shards(): lax.all_to_all(jnp.broadcast_to(chip, (chips,) + chip.shape), ('y', 'z'),...  23.8 us
    ppermute x3, waiting for transfers between devices, send(): return lax.ppermute(p, 'x', [(k, (k + shift) % n_dp) for k in range(n_dp)])  9.13 us
    pallas_call x1, Pallas kernels, shards(): pl.pallas_call(functools.partial(logits_kernel, scale), in_specs=[IN_HBM]...  5.13 us
    ppermute x3, starting transfers between devices, send(): return lax.ppermute(p, 'x', [(k, (k + shift) % n_dp) for k in range(n_dp)])  3.56 us
    pallas_call x1, Pallas kernels, shards(): pl.pallas_call(functools.partial(weights_kernel, first), in_specs=[IN_VME...  1.75 us
    pallas_call x1, Pallas kernels, shards(): pl.pallas_call(functools.partial(parts_kernel, others), in_specs=[IN_VMEM...  1.27 us
    ppermute x1, waiting for transfers between devices, shards(): other = lax.ppermute(lse, 'core', [(0, 1), (1, 0)])  1.16 us
  transfers between devices with their start and end apart: 4, of which 4 were waited for; matrix products, arithmetic and copies ran while one was open for 0% of the time, Pallas kernels for 4%

profile of v5, /device:TPU:38, one launch (start us, length us, event | category | flops | bytes accessed | tf_op | source)
XLA Modules:
  0.0 48.3 jit_solution(12406934721123727993)
XLA Ops:
  0.6 5.1 %shard_map.41 = (f32[512,2048]{1,0:T(8,128)S(1)}, f32[16,128]{1,0:T(8,128)S(1)}, bf16[2048,1024]{1,0:T(8,128)(2,1)S(1)}, bf16[512,256]{1,0:T(8,128)(2,1)S(1)}) custom-call(bf16[2048,1024]{1,0:T(8,128)(2,1)} %emb_hbm.1, bf16[512,1024]{1,0:T(8,128)(2,1)} %cent_hbm.1), custom_call_target="tpu_custom_call" | custom-call | tf_op jit(solution)/shard_map/pallas_call | solution.py:128
  5.8 0.1 collective-permute-start
  5.9 1.2 %collective-permute-done = f32[16,128]{1,0:T(8,128)S(1)} collective-permute-done((f32[16,128]{1,0:T(8,128)S(1)}, f32[16,128]{1,0:T(8,128)S(1)}, u32[]{:S(2)}, u32[]{:S(2)}) %collective-permute-start) | collective-permute-done | bytes 8224 | tf_op jit(solution)/shard_map/ppermute | solution.py:146
  7.1 23.8 %all_to_all.5.every_ref = f32[32,16,128]{2,1,0:T(8,128)S(1)} all-to-all(f32[32,16,128]{2,1,0:T(8,128)S(1)} %broadcast_in_dim.4), channel_id=1, replica_groups=mesh['x'=4,'z'=8,'y'=4,'core'=2] {'y','z'}, dimensions={0} | all-to-all | bytes 524288 | tf_op jit(solution)/shard_map/all_to_all | solution.py:149
  30.9 1.7 %shard_map.42 = (bf16[528,256]{1,0:T(8,128)(2,1)S(1)}, bf16[512,2048]{1,0:T(8,128)(2,1)S(1)}, bf16[16,256]{1,0:T(8,128)(2,1)S(1)}, f32[16,128]{1,0:T(8,128)}) custom-call(f32[512,2048]{1,0:T(8,128)S(1)} %get-tuple-element.14.z_ref, f32[32,16,128]{2,1,0:T(8,128)S(1)} %all_to_all.5.every_ref, bf16[2048,1024]{1,0:T(8,128)(2,1)S(1)} %get-tuple-element.16.emb_ref), custom_call_target="tpu_custom_call" | custom-call | tf_op jit(solution)/shard_map/pallas_call | solution.py:154
  32.6 1.4 %collective-permute-start.1 = (bf16[528,256]{1,0:T(8,128)(2,1)S(1)}, bf16[528,256]{1,0:T(8,128)(2,1)S(1)}, u32[]{:S(2)}, u32[]{:S(2)}) collective-permute-start(bf16[528,256]{1,0:T(8,128)(2,1)S(1)} %get-tuple-element.20), channel_id=1, source_target_pairs={{0,128},{64,192},{128,0},{192,64},{1,129},{65,193},{129,1},{193,65... | collective-permute-start | bytes 811016 | tf_op jit(solution)/shard_map/ppermute | solution.py:168
  34.0 1.3 %shard_map.44 = (bf16[528,256]{1,0:T(8,128)(2,1)S(1)}, bf16[528,256]{1,0:T(8,128)(2,1)S(1)}) custom-call(bf16[512,2048]{1,0:T(8,128)(2,1)S(1)} %get-tuple-element.17.w_ref, bf16[2048,1024]{1,0:T(8,128)(2,1)S(1)} %get-tuple-element.16.emb_ref, bf16[16,256]{1,0:T(8,128)(2,1)S(1)} %get-tuple-element.19.mass_ref), custom_call_target="tpu_custom_call" | custom-call | tf_op jit(solution)/shard_map/pallas_call | solution.py:170
  35.3 2.2 %collective-permute-start.2 = (bf16[528,256]{1,0:T(8,128)(2,1)S(1)}, bf16[528,256]{1,0:T(8,128)(2,1)S(1)}, u32[]{:S(2)}, u32[]{:S(2)}) collective-permute-start(bf16[528,256]{1,0:T(8,128)(2,1)S(1)} %get-tuple-element.23), channel_id=1, source_target_pairs={{0,64},{64,128},{128,192},{192,0},{1,65},{65,129},{129,193},{193,1... | collective-permute-start | bytes 811016 | tf_op jit(solution)/shard_map/ppermute | solution.py:168
  37.5 0.0 collective-permute-start.3
  37.5 6.1 %collective-permute-done.1.far_ref = bf16[528,256]{1,0:T(8,128)(2,1)S(1)} collective-permute-done((bf16[528,256]{1,0:T(8,128)(2,1)S(1)}, bf16[528,256]{1,0:T(8,128)(2,1)S(1)}, u32[]{:S(2)}, u32[]{:S(2)}) %collective-permute-start.1) | collective-permute-done | bytes 270368 | tf_op jit(solution)/shard_map/ppermute | solution.py:168
  43.5 0.7 %shard_map.43 = (f32[512,256]{1,0:T(8,128)S(1)}, f32[16,256]{1,0:T(8,128)S(1)}) custom-call(bf16[512,2048]{1,0:T(8,128)(2,1)S(1)} %get-tuple-element.17.w_ref, bf16[2048,1024]{1,0:T(8,128)(2,1)S(1)} %get-tuple-element.16.emb_ref, bf16[512,256]{1,0:T(8,128)(2,1)S(1)} %get-tuple-element.18.prior_ref, bf16[16,256]{1,0:T(8,128)(2,1)S(1)} %get-tuple-element.19.mass_ref, ...), custom_call_target="tpu_custom_call" | custom-call | tf_op jit(solution)/shard_map/pallas_call | solution.py:177
  44.3 0.7 %collective-permute-done.2.refs_0_ = bf16[528,256]{1,0:T(8,128)(2,1)S(1)} collective-permute-done((bf16[528,256]{1,0:T(8,128)(2,1)S(1)}, bf16[528,256]{1,0:T(8,128)(2,1)S(1)}, u32[]{:S(2)}, u32[]{:S(2)}) %collective-permute-start.2) | collective-permute-done | bytes 270368 | tf_op jit(solution)/shard_map/ppermute | solution.py:168
  45.0 2.4 %collective-permute-done.3.refs_1_ = bf16[528,256]{1,0:T(8,128)(2,1)S(1)} collective-permute-done((bf16[528,256]{1,0:T(8,128)(2,1)S(1)}, bf16[528,256]{1,0:T(8,128)(2,1)S(1)}, u32[]{:S(2)}, u32[]{:S(2)}) %collective-permute-start.3) | collective-permute-done | bytes 270368 | tf_op jit(solution)/shard_map/ppermute | solution.py:168
  47.3 0.9 %shard_map.45 = f32[512,256]{1,0:T(8,128)} custom-call(f32[512,256]{1,0:T(8,128)S(1)} %get-tuple-element.21.own_ref, f32[16,256]{1,0:T(8,128)S(1)} %get-tuple-element.22.mass_ref, bf16[528,256]{1,0:T(8,128)(2,1)S(1)} %collective-permute-done.2.refs_0_, bf16[528,256]{1,0:T(8,128)(2,1)S(1)} %collective-permute-done.3.refs_1_), custom_call_target="tpu_custom_call" | custom-call | tf_op jit(solution)/shard_map/pallas_call | solution.py:185
  (4 shorter events, 0.0 us)
Async XLA Ops:
  5.8 1.3 %collective-permute-start = (f32[16,128]{1,0:T(8,128)S(1)}, f32[16,128]{1,0:T(8,128)S(1)}, u32[]{:S(2)}, u32[]{:S(2)}) collective-permute-start(f32[16,128]{1,0:T(8,128)S(1)} %get-tuple-element.15), channel_id=1, source_target_pairs={{0,1},{1,0},{2,3},{3,2},{4,5},{5,4},{6,7},{7,6},{8,9},{9,8},{10,11... | collective-permute-start | bytes 24584 | tf_op jit(solution)/shard_map/ppermute | solution.py:146
  32.6 10.9 %collective-permute-start.1 = (bf16[528,256]{1,0:T(8,128)(2,1)S(1)}, bf16[528,256]{1,0:T(8,128)(2,1)S(1)}, u32[]{:S(2)}, u32[]{:S(2)}) collective-permute-start(bf16[528,256]{1,0:T(8,128)(2,1)S(1)} %get-tuple-element.20), channel_id=1, source_target_pairs={{0,128},{64,192},{128,0},{192,64},{1,129},{65,193},{129,1},{193,65... | collective-permute-start | bytes 811016 | tf_op jit(solution)/shard_map/ppermute | solution.py:168
  35.3 9.7 %collective-permute-start.2 = (bf16[528,256]{1,0:T(8,128)(2,1)S(1)}, bf16[528,256]{1,0:T(8,128)(2,1)S(1)}, u32[]{:S(2)}, u32[]{:S(2)}) collective-permute-start(bf16[528,256]{1,0:T(8,128)(2,1)S(1)} %get-tuple-element.23), channel_id=1, source_target_pairs={{0,64},{64,128},{128,192},{192,0},{1,65},{65,129},{129,193},{193,1... | collective-permute-start | bytes 811016 | tf_op jit(solution)/shard_map/ppermute | solution.py:168
  37.5 9.9 %collective-permute-start.3 = (bf16[528,256]{1,0:T(8,128)(2,1)S(1)}, bf16[528,256]{1,0:T(8,128)(2,1)S(1)}, u32[]{:S(2)}, u32[]{:S(2)}) collective-permute-start(bf16[528,256]{1,0:T(8,128)(2,1)S(1)} %get-tuple-element.24), channel_id=1, source_target_pairs={{0,192},{64,0},{128,64},{192,128},{1,193},{65,1},{129,65},{193,129... | collective-permute-start | bytes 811016 | tf_op jit(solution)/shard_map/ppermute | solution.py:168

commit v6 on v5

--- a/solution.py
+++ b/solution.py
@@ -13,8 +13,9 @@
 LOG2E = math.log2(math.e)
 LN2 = math.log(2.0)
 ROWS = 256
-LOADS = 2
+FIRST_LOAD = 512
 LANES = 128
+EXCHANGE = ("y", "z_lo", "z_hi")
 MASS_ROWS = 16
 VMEM_LIMIT = 16 * 1024 * 1024
 IN_VMEM = pl.BlockSpec(memory_space=pltpu.VMEM)
@@ -32,22 +33,22 @@
 def logits_kernel(scale, emb_hbm, cent_hbm, z_ref, lse_ref, emb_ref, prior_ref, cent_ref, half_sq, sems):
     rows = emb_ref.shape[0]
     cols = prior_ref.shape[1]
-    cent_copy = pltpu.make_async_copy(cent_hbm, cent_ref, sems.at[LOADS])
+    cent_copy = pltpu.make_async_copy(cent_hbm, cent_ref, sems.at[0])
     cent_copy.start()
-    load = rows // LOADS
-    copies = []
-    for k in range(LOADS):
-        part = pl.ds(k * load, load)
-        copies.append(pltpu.make_async_copy(emb_hbm.at[part, :], emb_ref.at[part, :], sems.at[k]))
-        copies[-1].start()
+    copies = {}
+    for start, end in ((0, FIRST_LOAD), (FIRST_LOAD, rows)):
+        part = pl.ds(start, end - start)
+        sem = sems.at[1 + len(copies)]
+        copies[start] = pltpu.make_async_copy(emb_hbm.at[part, :], emb_ref.at[part, :], sem)
+        copies[start].start()
     cent_copy.wait()
     c = cent_ref[...].astype(jnp.float32)
     half_sq[...] = jnp.broadcast_to(0.5 * jnp.sum(c * c, axis=1, keepdims=True), half_sq.shape)
     first_col = pl.multiple_of(lax.axis_index("x") * cols, cols)
     prior_ref[...] = cent_ref[:, pl.ds(first_col, cols)]
     for r in range(0, rows, ROWS):
-        if r % load == 0:
-            copies[r // load].wait()
+        if r in copies:
+            copies[r].wait()
         inner = lax.dot_general(
             cent_ref[...], emb_ref[r : r + ROWS, :], (((1,), (1,)), ((), ())), preferred_element_type=jnp.float32
         )
@@ -138,15 +139,15 @@
         scratch_shapes=[
             pltpu.VMEM(cent.shape, cent.dtype),
             pltpu.VMEM((cents, LANES), jnp.float32),
-            pltpu.SemaphoreType.DMA((LOADS + 1,)),
+            pltpu.SemaphoreType.DMA((3,)),
         ],
         compiler_params=params,
     )(in_hbm(emb), in_hbm(cent))
 
     other = lax.ppermute(lse, "core", [(0, 1), (1, 0)])
     chip = merge(jnp.stack([lse, other]))
-    chips = lax.axis_size("z") * lax.axis_size("y")
-    every = lax.all_to_all(jnp.broadcast_to(chip, (chips,) + chip.shape), ("y", "z"), 0, 0)
+    chips = math.prod(lax.axis_size(axis) for axis in EXCHANGE)
+    every = lax.all_to_all(jnp.broadcast_to(chip, (chips,) + chip.shape), EXCHANGE, 0, 0)
 
     part = pltpu.VMEM((cents + MASS_ROWS, cols), jnp.bfloat16)
     first = n_dp // 2
@@ -194,8 +195,8 @@
 
 def solution(mesh):
     n_dp = mesh.shape["dp"]
-    fine = Mesh(mesh.devices.reshape(n_dp, 8, 4, 2), ("x", "z", "y", "core"))
-    cent = ("z", "y", "core")
+    fine = Mesh(mesh.devices.reshape(n_dp, 4, 2, 4, 2), ("x", "z_hi", "z_lo", "y", "core"))
+    cent = ("z_hi", "z_lo", "y", "core")
     return jax.shard_map(
         functools.partial(shards, n_dp),
         mesh=fine,

time: 48.4 us -> 47.5 us (0.981)
  transfers between devices with their start and end apart: 4 -> 4, of which waited for: 4 -> 3; matrix products, arithmetic and copies ran while one was open for 0% -> 0% of each run, Pallas kernels for 4% -> 4%
where the time goes in v6:
time: 47.5 us; the launch traced here: 47.3 us
  blocking collectives  23.5 us (49%)
  waiting for transfers between devices  9.94 us (21%)
  Pallas kernels  9.49 us (20%)
  starting transfers between devices  3.65 us (8%)
  between operations  0.69 us (1%)
    all_to_all x1, blocking collectives, shards(): lax.all_to_all(jnp.broadcast_to(chip, (chips,) + chip.shape), EXCHANGE, 0...  23.5 us
    ppermute x3, waiting for transfers between devices, send(): return lax.ppermute(p, 'x', [(k, (k + shift) % n_dp) for k in range(n_dp)])  8.78 us
    pallas_call x1, Pallas kernels, shards(): pl.pallas_call(functools.partial(logits_kernel, scale), in_specs=[IN_HBM]...  4.8 us
    ppermute x3, starting transfers between devices, send(): return lax.ppermute(p, 'x', [(k, (k + shift) % n_dp) for k in range(n_dp)])  3.56 us
    pallas_call x1, Pallas kernels, shards(): pl.pallas_call(functools.partial(weights_kernel, first), in_specs=[IN_VME...  1.75 us
    pallas_call x1, Pallas kernels, shards(): pl.pallas_call(functools.partial(parts_kernel, others), in_specs=[IN_VMEM...  1.27 us
    ppermute x1, waiting for transfers between devices, shards(): other = lax.ppermute(lse, 'core', [(0, 1), (1, 0)])  1.16 us
  transfers between devices with their start and end apart: 4, of which 3 were waited for; matrix products, arithmetic and copies ran while one was open for 0% of the time, Pallas kernels for 4%

profile of v6, /device:TPU:38, one launch (start us, length us, event | category | flops | bytes accessed | tf_op | source)
XLA Modules:
  0.0 47.3 jit_solution(9018127558815831608)
XLA Ops:
  0.6 4.8 %shard_map.41 = (f32[512,2048]{1,0:T(8,128)S(1)}, f32[16,128]{1,0:T(8,128)S(1)}, bf16[2048,1024]{1,0:T(8,128)(2,1)S(1)}, bf16[512,256]{1,0:T(8,128)(2,1)S(1)}) custom-call(bf16[2048,1024]{1,0:T(8,128)(2,1)} %emb_hbm.1, bf16[512,1024]{1,0:T(8,128)(2,1)} %cent_hbm.1), custom_call_target="tpu_custom_call" | custom-call | tf_op jit(solution)/shard_map/pallas_call | solution.py:129
  5.4 0.1 collective-permute-start
  5.5 1.2 %collective-permute-done = f32[16,128]{1,0:T(8,128)S(1)} collective-permute-done((f32[16,128]{1,0:T(8,128)S(1)}, f32[16,128]{1,0:T(8,128)S(1)}, u32[]{:S(2)}, u32[]{:S(2)}) %collective-permute-start) | collective-permute-done | bytes 8224 | tf_op jit(solution)/shard_map/ppermute | solution.py:147
  6.8 23.5 %all_to_all.5.every_ref = f32[32,16,128]{2,1,0:T(8,128)S(1)} all-to-all(f32[32,16,128]{2,1,0:T(8,128)S(1)} %broadcast_in_dim.4), channel_id=1, replica_groups=mesh['x'=4,'z_hi'=4,'z_lo'=2,'y'=4,'core'=2] {'y','z_lo','z_hi'}, dimensions={0} | all-to-all | bytes 524288 | tf_op jit(solution)/shard_map/all_to_all | solution.py:150
  30.3 1.7 %shard_map.42 = (bf16[528,256]{1,0:T(8,128)(2,1)S(1)}, bf16[512,2048]{1,0:T(8,128)(2,1)S(1)}, bf16[16,256]{1,0:T(8,128)(2,1)S(1)}, f32[16,128]{1,0:T(8,128)}) custom-call(f32[512,2048]{1,0:T(8,128)S(1)} %get-tuple-element.14.z_ref, f32[32,16,128]{2,1,0:T(8,128)S(1)} %all_to_all.5.every_ref, bf16[2048,1024]{1,0:T(8,128)(2,1)S(1)} %get-tuple-element.16.emb_ref), custom_call_target="tpu_custom_call" | custom-call | tf_op jit(solution)/shard_map/pallas_call | solution.py:155
  32.0 1.4 %collective-permute-start.1 = (bf16[528,256]{1,0:T(8,128)(2,1)S(1)}, bf16[528,256]{1,0:T(8,128)(2,1)S(1)}, u32[]{:S(2)}, u32[]{:S(2)}) collective-permute-start(bf16[528,256]{1,0:T(8,128)(2,1)S(1)} %get-tuple-element.20), channel_id=1, source_target_pairs={{0,128},{64,192},{128,0},{192,64},{1,129},{65,193},{129,1},{193,65... | collective-permute-start | bytes 811016 | tf_op jit(solution)/shard_map/ppermute | solution.py:169
  33.4 1.3 %shard_map.44 = (bf16[528,256]{1,0:T(8,128)(2,1)S(1)}, bf16[528,256]{1,0:T(8,128)(2,1)S(1)}) custom-call(bf16[512,2048]{1,0:T(8,128)(2,1)S(1)} %get-tuple-element.17.w_ref, bf16[2048,1024]{1,0:T(8,128)(2,1)S(1)} %get-tuple-element.16.emb_ref, bf16[16,256]{1,0:T(8,128)(2,1)S(1)} %get-tuple-element.19.mass_ref), custom_call_target="tpu_custom_call" | custom-call | tf_op jit(solution)/shard_map/pallas_call | solution.py:171
  34.7 2.2 %collective-permute-start.2 = (bf16[528,256]{1,0:T(8,128)(2,1)S(1)}, bf16[528,256]{1,0:T(8,128)(2,1)S(1)}, u32[]{:S(2)}, u32[]{:S(2)}) collective-permute-start(bf16[528,256]{1,0:T(8,128)(2,1)S(1)} %get-tuple-element.23), channel_id=1, source_target_pairs={{0,64},{64,128},{128,192},{192,0},{1,65},{65,129},{129,193},{193,1... | collective-permute-start | bytes 811016 | tf_op jit(solution)/shard_map/ppermute | solution.py:169
  36.9 0.0 collective-permute-start.3
  36.9 6.1 %collective-permute-done.1.far_ref = bf16[528,256]{1,0:T(8,128)(2,1)S(1)} collective-permute-done((bf16[528,256]{1,0:T(8,128)(2,1)S(1)}, bf16[528,256]{1,0:T(8,128)(2,1)S(1)}, u32[]{:S(2)}, u32[]{:S(2)}) %collective-permute-start.1) | collective-permute-done | bytes 270368 | tf_op jit(solution)/shard_map/ppermute | solution.py:169
  42.9 0.7 %shard_map.43 = (f32[512,256]{1,0:T(8,128)S(1)}, f32[16,256]{1,0:T(8,128)S(1)}) custom-call(bf16[512,2048]{1,0:T(8,128)(2,1)S(1)} %get-tuple-element.17.w_ref, bf16[2048,1024]{1,0:T(8,128)(2,1)S(1)} %get-tuple-element.16.emb_ref, bf16[512,256]{1,0:T(8,128)(2,1)S(1)} %get-tuple-element.18.prior_ref, bf16[16,256]{1,0:T(8,128)(2,1)S(1)} %get-tuple-element.19.mass_ref, ...), custom_call_target="tpu_custom_call" | custom-call | tf_op jit(solution)/shard_map/pallas_call | solution.py:178
  43.7 0.0 collective-permute-done.2.refs_0_
  43.7 2.7 %collective-permute-done.3.refs_1_ = bf16[528,256]{1,0:T(8,128)(2,1)S(1)} collective-permute-done((bf16[528,256]{1,0:T(8,128)(2,1)S(1)}, bf16[528,256]{1,0:T(8,128)(2,1)S(1)}, u32[]{:S(2)}, u32[]{:S(2)}) %collective-permute-start.3) | collective-permute-done | bytes 270368 | tf_op jit(solution)/shard_map/ppermute | solution.py:169
  46.4 0.9 %shard_map.45 = f32[512,256]{1,0:T(8,128)} custom-call(f32[512,256]{1,0:T(8,128)S(1)} %get-tuple-element.21.own_ref, f32[16,256]{1,0:T(8,128)S(1)} %get-tuple-element.22.mass_ref, bf16[528,256]{1,0:T(8,128)(2,1)S(1)} %collective-permute-done.2.refs_0_, bf16[528,256]{1,0:T(8,128)(2,1)S(1)} %collective-permute-done.3.refs_1_), custom_call_target="tpu_custom_call" | custom-call | tf_op jit(solution)/shard_map/pallas_call | solution.py:186
  (4 shorter events, 0.0 us)
Async XLA Ops:
  5.4 1.3 %collective-permute-start = (f32[16,128]{1,0:T(8,128)S(1)}, f32[16,128]{1,0:T(8,128)S(1)}, u32[]{:S(2)}, u32[]{:S(2)}) collective-permute-start(f32[16,128]{1,0:T(8,128)S(1)} %get-tuple-element.15), channel_id=1, source_target_pairs={{0,1},{1,0},{2,3},{3,2},{4,5},{5,4},{6,7},{7,6},{8,9},{9,8},{10,11... | collective-permute-start | bytes 24584 | tf_op jit(solution)/shard_map/ppermute | solution.py:147
  32.0 10.9 %collective-permute-start.1 = (bf16[528,256]{1,0:T(8,128)(2,1)S(1)}, bf16[528,256]{1,0:T(8,128)(2,1)S(1)}, u32[]{:S(2)}, u32[]{:S(2)}) collective-permute-start(bf16[528,256]{1,0:T(8,128)(2,1)S(1)} %get-tuple-element.20), channel_id=1, source_target_pairs={{0,128},{64,192},{128,0},{192,64},{1,129},{65,193},{129,1},{193,65... | collective-permute-start | bytes 811016 | tf_op jit(solution)/shard_map/ppermute | solution.py:169
  34.7 9.0 %collective-permute-start.2 = (bf16[528,256]{1,0:T(8,128)(2,1)S(1)}, bf16[528,256]{1,0:T(8,128)(2,1)S(1)}, u32[]{:S(2)}, u32[]{:S(2)}) collective-permute-start(bf16[528,256]{1,0:T(8,128)(2,1)S(1)} %get-tuple-element.23), channel_id=1, source_target_pairs={{0,64},{64,128},{128,192},{192,0},{1,65},{65,129},{129,193},{193,1... | collective-permute-start | bytes 811016 | tf_op jit(solution)/shard_map/ppermute | solution.py:169
  36.9 9.5 %collective-permute-start.3 = (bf16[528,256]{1,0:T(8,128)(2,1)S(1)}, bf16[528,256]{1,0:T(8,128)(2,1)S(1)}, u32[]{:S(2)}, u32[]{:S(2)}) collective-permute-start(bf16[528,256]{1,0:T(8,128)(2,1)S(1)} %get-tuple-element.24), channel_id=1, source_target_pairs={{0,192},{64,0},{128,64},{192,128},{1,193},{65,1},{129,65},{193,129... | collective-permute-start | bytes 811016 | tf_op jit(solution)/shard_map/ppermute | solution.py:169

commit v7 on v6

--- a/solution.py
+++ b/solution.py
@@ -30,7 +30,7 @@
     return pltpu.with_memory_space_constraint(x, pltpu.HBM)
 
 
-def logits_kernel(scale, emb_hbm, cent_hbm, z_ref, lse_ref, emb_ref, prior_ref, cent_ref, half_sq, sems):
+def logits_kernel(scale, emb_hbm, cent_hbm, p_ref, top_ref, lse_ref, emb_ref, prior_ref, cent_ref, half_sq, sems):
     rows = emb_ref.shape[0]
     cols = prior_ref.shape[1]
     cent_copy = pltpu.make_async_copy(cent_hbm, cent_ref, sems.at[0])
@@ -53,10 +53,12 @@
             cent_ref[...], emb_ref[r : r + ROWS, :], (((1,), (1,)), ((), ())), preferred_element_type=jnp.float32
         )
         z = (inner - half_sq[:, :1]) * scale
-        z_ref[:, r : r + ROWS] = z
         top = jnp.max(z, axis=0, keepdims=True)
-        lse = top + jnp.log2(jnp.sum(jnp.exp2(z - top), axis=0, keepdims=True))
+        p = jnp.exp2(z - top)
+        p_ref[:, r : r + ROWS] = p
+        lse = top + jnp.log2(jnp.sum(p, axis=0, keepdims=True))
         for k in range(ROWS // LANES):
+            top_ref[pl.ds(r // LANES + k, 1), :] = top[:, k * LANES : (k + 1) * LANES]
             lse_ref[pl.ds(r // LANES + k, 1), :] = lse[:, k * LANES : (k + 1) * LANES]
 
 
@@ -65,42 +67,42 @@
     return top + jnp.log2(jnp.sum(jnp.exp2(lse - top), axis=0))
 
 
-def weights_kernel(shift, z_ref, every_ref, emb_ref, part_ref, w_ref, mass_ref, log_totals_ref):
-    cents, rows = z_ref.shape
+def weights_kernel(shift, p_ref, top_ref, every_ref, emb_ref, part_ref, w_ref, mass_ref, log_totals_ref):
+    cents, rows = p_ref.shape
+    cols = mass_ref.shape[1]
     totals = merge(every_ref[...])
     log_totals_ref[...] = totals * LN2
+    factor = jnp.exp2(top_ref[...] - totals)
     mass = jnp.zeros((cents, LANES), jnp.float32)
     for k in range(rows // LANES):
-        w = jnp.exp2(z_ref[:, k * LANES : (k + 1) * LANES] - totals[k : k + 1, :])
+        w = p_ref[:, k * LANES : (k + 1) * LANES] * factor[k : k + 1, :]
         w_ref[:, k * LANES : (k + 1) * LANES] = w.astype(jnp.bfloat16)
         mass = mass + w
-    cols = mass_ref.shape[1]
+    part_ref[:cents, :] = part_product(shift, w_ref, emb_ref).astype(jnp.bfloat16)
     mass = jnp.broadcast_to(jnp.sum(mass, axis=1, keepdims=True), (cents, LANES)).T
     half = MASS_ROWS // 2
-    mass_ref[...] = jnp.concatenate([mass[:half, :cols], mass[:half, cols:]], axis=0).astype(jnp.bfloat16)
-    part_product(shift, w_ref, emb_ref, mass_ref, part_ref)
-
-
-def part_product(shift, w_ref, emb_ref, mass_ref, part_ref):
+    mass = jnp.concatenate([mass[:half, :cols], mass[:half, cols:]], axis=0).astype(jnp.bfloat16)
+    mass_ref[...] = mass
+    part_ref[cents:, :] = mass
+
+
+def part_product(shift, w_ref, emb_ref):
+    n_dp = lax.axis_size("x")
+    cols = emb_ref.shape[1] // n_dp
+    first_col = pl.multiple_of(lax.rem(lax.axis_index("x") + shift, n_dp) * cols, cols)
+    return jnp.dot(w_ref[...], emb_ref[:, pl.ds(first_col, cols)], preferred_element_type=jnp.float32)
+
+
+def parts_kernel(shifts, w_ref, emb_ref, mass_ref, *parts_refs):
     cents = w_ref.shape[0]
-    cols = mass_ref.shape[1]
-    n_dp = emb_ref.shape[1] // cols
-    first_col = pl.multiple_of(lax.rem(lax.axis_index("x") + shift, n_dp) * cols, cols)
-    part_ref[:cents, :] = jnp.dot(
-        w_ref[...], emb_ref[:, pl.ds(first_col, cols)], preferred_element_type=jnp.float32
-    ).astype(jnp.bfloat16)
-    part_ref[cents:, :] = mass_ref[...]
-
-
-def parts_kernel(shifts, w_ref, emb_ref, mass_ref, *parts_refs):
     for shift, part_ref in zip(shifts, parts_refs):
-        part_product(shift, w_ref, emb_ref, mass_ref, part_ref)
+        part_ref[:cents, :] = part_product(shift, w_ref, emb_ref).astype(jnp.bfloat16)
+        part_ref[cents:, :] = mass_ref[...]
 
 
 def own_kernel(w_ref, emb_ref, prior_ref, mass_ref, far_ref, out_ref, out_mass_ref):
-    cents, cols = out_ref.shape
-    first_col = pl.multiple_of(lax.axis_index("x") * cols, cols)
-    own = jnp.dot(w_ref[...], emb_ref[:, pl.ds(first_col, cols)], preferred_element_type=jnp.float32)
+    cents = out_ref.shape[0]
+    own = part_product(0, w_ref, emb_ref)
     out_ref[...] = own + PRIOR * prior_ref[...].astype(jnp.float32) + far_ref[:cents, :].astype(jnp.float32)
     out_mass_ref[...] = PRIOR + mass_ref[...].astype(jnp.float32) + far_ref[cents:, :].astype(jnp.float32)
 
@@ -126,12 +128,13 @@
     cols = width // n_dp
     scale = 2.0 * LOG2E / (SOFTNESS * math.sqrt(width))
     params = pltpu.CompilerParams(vmem_limit_bytes=VMEM_LIMIT)
-    z, lse, emb_vmem, prior = pl.pallas_call(
+    p, top, lse, emb_vmem, prior = pl.pallas_call(
         functools.partial(logits_kernel, scale),
         in_specs=[IN_HBM] * 2,
-        out_specs=[IN_VMEM] * 4,
+        out_specs=[IN_VMEM] * 5,
         out_shape=[
             pltpu.VMEM((cents, rows), jnp.float32),
+            pltpu.VMEM((rows // LANES, LANES), jnp.float32),
             pltpu.VMEM((rows // LANES, LANES), jnp.float32),
             pltpu.VMEM(emb.shape, emb.dtype),
             pltpu.VMEM((cents, cols), cent.dtype),
@@ -154,7 +157,7 @@
     others = [k for k in range(1, n_dp) if k != first]
     far, w, mass, log_totals = pl.pallas_call(
         functools.partial(weights_kernel, first),
-        in_specs=[IN_VMEM] * 3,
+        in_specs=[IN_VMEM] * 4,
         out_specs=[IN_VMEM] * 4,
         out_shape=[
             part,
@@ -163,7 +166,7 @@
             jax.ShapeDtypeStruct(lse.shape, jnp.float32),
         ],
         compiler_params=params,
-    )(in_vmem(z), in_vmem(every), in_vmem(emb_vmem))
+    )(in_vmem(p), in_vmem(top), in_vmem(every), in_vmem(emb_vmem))
 
     def send(p, shift):
         return lax.ppermute(p, "x", [(k, (k + shift) % n_dp) for k in range(n_dp)])

time: 47.5 us -> 47.3 us (level)
  no operation moved by 1% of the time
where the time goes in v7:
time: 47.3 us; the launch traced here: 47.1 us
  blocking collectives  23.5 us (50%)
  waiting for transfers between devices  9.91 us (21%)
  Pallas kernels  9.29 us (20%)
  starting transfers between devices  3.69 us (8%)
  between operations  0.69 us (1%)
    all_to_all x1, blocking collectives, shards(): lax.all_to_all(jnp.broadcast_to(chip, (chips,) + chip.shape), EXCHANGE, 0...  23.5 us
    ppermute x3, waiting for transfers between devices, send(): return lax.ppermute(p, 'x', [(k, (k + shift) % n_dp) for k in range(n_dp)])  8.75 us
    pallas_call x1, Pallas kernels, shards(): pl.pallas_call(functools.partial(logits_kernel, scale), in_specs=[IN_HBM]...  4.87 us
    ppermute x3, starting transfers between devices, send(): return lax.ppermute(p, 'x', [(k, (k + shift) % n_dp) for k in range(n_dp)])  3.59 us
    pallas_call x1, Pallas kernels, shards(): pl.pallas_call(functools.partial(weights_kernel, first), in_specs=[IN_VME...  1.48 us
    pallas_call x1, Pallas kernels, shards(): pl.pallas_call(functools.partial(parts_kernel, others), in_specs=[IN_VMEM...  1.27 us
    ppermute x1, waiting for transfers between devices, shards(): other = lax.ppermute(lse, 'core', [(0, 1), (1, 0)])  1.16 us
  transfers between devices with their start and end apart: 4, of which 3 were waited for; matrix products, arithmetic and copies ran while one was open for 0% of the time, Pallas kernels for 4%

profile of v7, /device:TPU:38, one launch (start us, length us, event | category | flops | bytes accessed | tf_op | source)
XLA Modules:
  0.0 47.1 jit_solution(13464062677846582374)
XLA Ops:
  0.6 4.9 %shard_map.41 = (f32[512,2048]{1,0:T(8,128)S(1)}, f32[16,128]{1,0:T(8,128)S(1)}, f32[16,128]{1,0:T(8,128)S(1)}, bf16[2048,1024]{1,0:T(8,128)(2,1)S(1)}, bf16[512,256]{1,0:T(8,128)(2,1)S(1)}) custom-call(bf16[2048,1024]{1,0:T(8,128)(2,1)} %emb_hbm.1, bf16[512,1024]{1,0:T(8,128)(2,1)} %cent_hbm.1), custom_call_target="tpu_custom_call" | custom-call | tf_op jit(solution)/shard_map/pallas_call | solution.py:131
  5.5 0.1 collective-permute-start
  5.6 1.2 %collective-permute-done = f32[16,128]{1,0:T(8,128)S(1)} collective-permute-done((f32[16,128]{1,0:T(8,128)S(1)}, f32[16,128]{1,0:T(8,128)S(1)}, u32[]{:S(2)}, u32[]{:S(2)}) %collective-permute-start) | collective-permute-done | bytes 8224 | tf_op jit(solution)/shard_map/ppermute | solution.py:150
  6.8 23.5 %all_to_all.5.every_ref = f32[32,16,128]{2,1,0:T(8,128)S(1)} all-to-all(f32[32,16,128]{2,1,0:T(8,128)S(1)} %broadcast_in_dim.4), channel_id=1, replica_groups=mesh['x'=4,'z_hi'=4,'z_lo'=2,'y'=4,'core'=2] {'y','z_lo','z_hi'}, dimensions={0} | all-to-all | bytes 524288 | tf_op jit(solution)/shard_map/all_to_all | solution.py:153
  30.3 1.5 %shard_map.42 = (bf16[528,256]{1,0:T(8,128)(2,1)S(1)}, bf16[512,2048]{1,0:T(8,128)(2,1)S(1)}, bf16[16,256]{1,0:T(8,128)(2,1)S(1)}, f32[16,128]{1,0:T(8,128)}) custom-call(f32[512,2048]{1,0:T(8,128)S(1)} %get-tuple-element.15.p_ref, f32[16,128]{1,0:T(8,128)S(1)} %get-tuple-element.16.top_ref, f32[32,16,128]{2,1,0:T(8,128)S(1)} %all_to_all.5.every_ref, ...), custom_call_target="tpu_custom_call" | custom-call | tf_op jit(solution)/shard_map/pallas_call | solution.py:158
  31.8 1.4 %collective-permute-start.1 = (bf16[528,256]{1,0:T(8,128)(2,1)S(1)}, bf16[528,256]{1,0:T(8,128)(2,1)S(1)}, u32[]{:S(2)}, u32[]{:S(2)}) collective-permute-start(bf16[528,256]{1,0:T(8,128)(2,1)S(1)} %get-tuple-element.22), channel_id=1, source_target_pairs={{0,128},{64,192},{128,0},{192,64},{1,129},{65,193},{129,1},{193,65... | collective-permute-start | bytes 811016 | tf_op jit(solution)/shard_map/ppermute | solution.py:172
  33.2 1.3 %shard_map.44 = (bf16[528,256]{1,0:T(8,128)(2,1)S(1)}, bf16[528,256]{1,0:T(8,128)(2,1)S(1)}) custom-call(bf16[512,2048]{1,0:T(8,128)(2,1)S(1)} %get-tuple-element.19.w_ref, bf16[2048,1024]{1,0:T(8,128)(2,1)S(1)} %get-tuple-element.18.emb_ref, bf16[16,256]{1,0:T(8,128)(2,1)S(1)} %get-tuple-element.21.mass_ref), custom_call_target="tpu_custom_call" | custom-call | tf_op jit(solution)/shard_map/pallas_call | solution.py:174
  34.5 2.2 %collective-permute-start.2 = (bf16[528,256]{1,0:T(8,128)(2,1)S(1)}, bf16[528,256]{1,0:T(8,128)(2,1)S(1)}, u32[]{:S(2)}, u32[]{:S(2)}) collective-permute-start(bf16[528,256]{1,0:T(8,128)(2,1)S(1)} %get-tuple-element.25), channel_id=1, source_target_pairs={{0,64},{64,128},{128,192},{192,0},{1,65},{65,129},{129,193},{193,1... | collective-permute-start | bytes 811016 | tf_op jit(solution)/shard_map/ppermute | solution.py:172
  36.7 0.0 collective-permute-start.3
  36.7 6.1 %collective-permute-done.1.far_ref = bf16[528,256]{1,0:T(8,128)(2,1)S(1)} collective-permute-done((bf16[528,256]{1,0:T(8,128)(2,1)S(1)}, bf16[528,256]{1,0:T(8,128)(2,1)S(1)}, u32[]{:S(2)}, u32[]{:S(2)}) %collective-permute-start.1) | collective-permute-done | bytes 270368 | tf_op jit(solution)/shard_map/ppermute | solution.py:172
  42.7 0.7 %shard_map.43 = (f32[512,256]{1,0:T(8,128)S(1)}, f32[16,256]{1,0:T(8,128)S(1)}) custom-call(bf16[512,2048]{1,0:T(8,128)(2,1)S(1)} %get-tuple-element.19.w_ref, bf16[2048,1024]{1,0:T(8,128)(2,1)S(1)} %get-tuple-element.18.emb_ref, bf16[512,256]{1,0:T(8,128)(2,1)S(1)} %get-tuple-element.20.prior_ref, bf16[16,256]{1,0:T(8,128)(2,1)S(1)} %get-tuple-element.21.mass_ref, ...), custom_call_target="tpu_custom_call" | custom-call | tf_op jit(solution)/shard_map/pallas_call | solution.py:181
  43.5 0.0 collective-permute-done.2.refs_0_
  43.5 2.7 %collective-permute-done.3.refs_1_ = bf16[528,256]{1,0:T(8,128)(2,1)S(1)} collective-permute-done((bf16[528,256]{1,0:T(8,128)(2,1)S(1)}, bf16[528,256]{1,0:T(8,128)(2,1)S(1)}, u32[]{:S(2)}, u32[]{:S(2)}) %collective-permute-start.3) | collective-permute-done | bytes 270368 | tf_op jit(solution)/shard_map/ppermute | solution.py:172
  46.2 0.9 %shard_map.45 = f32[512,256]{1,0:T(8,128)} custom-call(f32[512,256]{1,0:T(8,128)S(1)} %get-tuple-element.23.own_ref, f32[16,256]{1,0:T(8,128)S(1)} %get-tuple-element.24.mass_ref, bf16[528,256]{1,0:T(8,128)(2,1)S(1)} %collective-permute-done.2.refs_0_, bf16[528,256]{1,0:T(8,128)(2,1)S(1)} %collective-permute-done.3.refs_1_), custom_call_target="tpu_custom_call" | custom-call | tf_op jit(solution)/shard_map/pallas_call | solution.py:189
  (4 shorter events, 0.0 us)
Async XLA Ops:
  5.5 1.3 %collective-permute-start = (f32[16,128]{1,0:T(8,128)S(1)}, f32[16,128]{1,0:T(8,128)S(1)}, u32[]{:S(2)}, u32[]{:S(2)}) collective-permute-start(f32[16,128]{1,0:T(8,128)S(1)} %get-tuple-element.17), channel_id=1, source_target_pairs={{0,1},{1,0},{2,3},{3,2},{4,5},{5,4},{6,7},{7,6},{8,9},{9,8},{10,11... | collective-permute-start | bytes 24584 | tf_op jit(solution)/shard_map/ppermute | solution.py:150
  31.8 10.9 %collective-permute-start.1 = (bf16[528,256]{1,0:T(8,128)(2,1)S(1)}, bf16[528,256]{1,0:T(8,128)(2,1)S(1)}, u32[]{:S(2)}, u32[]{:S(2)}) collective-permute-start(bf16[528,256]{1,0:T(8,128)(2,1)S(1)} %get-tuple-element.22), channel_id=1, source_target_pairs={{0,128},{64,192},{128,0},{192,64},{1,129},{65,193},{129,1},{193,65... | collective-permute-start | bytes 811016 | tf_op jit(solution)/shard_map/ppermute | solution.py:172
  34.5 9.0 %collective-permute-start.2 = (bf16[528,256]{1,0:T(8,128)(2,1)S(1)}, bf16[528,256]{1,0:T(8,128)(2,1)S(1)}, u32[]{:S(2)}, u32[]{:S(2)}) collective-permute-start(bf16[528,256]{1,0:T(8,128)(2,1)S(1)} %get-tuple-element.25), channel_id=1, source_target_pairs={{0,64},{64,128},{128,192},{192,0},{1,65},{65,129},{129,193},{193,1... | collective-permute-start | bytes 811016 | tf_op jit(solution)/shard_map/ppermute | solution.py:172
  36.7 9.5 %collective-permute-start.3 = (bf16[528,256]{1,0:T(8,128)(2,1)S(1)}, bf16[528,256]{1,0:T(8,128)(2,1)S(1)}, u32[]{:S(2)}, u32[]{:S(2)}) collective-permute-start(bf16[528,256]{1,0:T(8,128)(2,1)S(1)} %get-tuple-element.26), channel_id=1, source_target_pairs={{0,192},{64,0},{128,64},{192,128},{1,193},{65,1},{129,65},{193,129... | collective-permute-start | bytes 811016 | tf_op jit(solution)/shard_map/ppermute | solution.py:172

commit v8 on v7

--- a/solution.py
+++ b/solution.py
@@ -12,7 +12,7 @@
 PRIOR = 4.0
 LOG2E = math.log2(math.e)
 LN2 = math.log(2.0)
-ROWS = 256
+ROWS = 512
 FIRST_LOAD = 512
 LANES = 128
 EXCHANGE = ("y", "z_lo", "z_hi")
@@ -148,7 +148,8 @@
     )(in_hbm(emb), in_hbm(cent))
 
     other = lax.ppermute(lse, "core", [(0, 1), (1, 0)])
-    chip = merge(jnp.stack([lse, other]))
+    top_lse = jnp.maximum(lse, other)
+    chip = top_lse + jnp.log2(1.0 + jnp.exp2(jnp.minimum(lse, other) - top_lse))
     chips = math.prod(lax.axis_size(axis) for axis in EXCHANGE)
     every = lax.all_to_all(jnp.broadcast_to(chip, (chips,) + chip.shape), EXCHANGE, 0, 0)
 

time: 47.3 us -> 47.2 us (level)
  no operation moved by 1% of the time
where the time goes in v8:
time: 47.2 us; the launch traced here: 47.1 us
  blocking collectives  23.5 us (50%)
  waiting for transfers between devices  9.91 us (21%)
  Pallas kernels  9.28 us (20%)
  starting transfers between devices  3.69 us (8%)
  between operations  0.68 us (1%)
    all_to_all x1, blocking collectives, shards(): lax.all_to_all(jnp.broadcast_to(chip, (chips,) + chip.shape), EXCHANGE, 0...  23.5 us
    ppermute x3, waiting for transfers between devices, send(): return lax.ppermute(p, 'x', [(k, (k + shift) % n_dp) for k in range(n_dp)])  8.75 us
    pallas_call x1, Pallas kernels, shards(): pl.pallas_call(functools.partial(logits_kernel, scale), in_specs=[IN_HBM]...  4.85 us
    ppermute x3, starting transfers between devices, send(): return lax.ppermute(p, 'x', [(k, (k + shift) % n_dp) for k in range(n_dp)])  3.59 us
    pallas_call x1, Pallas kernels, shards(): pl.pallas_call(functools.partial(weights_kernel, first), in_specs=[IN_VME...  1.48 us
    pallas_call x1, Pallas kernels, shards(): pl.pallas_call(functools.partial(parts_kernel, others), in_specs=[IN_VMEM...  1.27 us
    ppermute x1, waiting for transfers between devices, shards(): other = lax.ppermute(lse, 'core', [(0, 1), (1, 0)])  1.16 us
  transfers between devices with their start and end apart: 4, of which 3 were waited for; matrix products, arithmetic and copies ran while one was open for 0% of the time, Pallas kernels for 4%

profile of v8, /device:TPU:38, one launch (start us, length us, event | category | flops | bytes accessed | tf_op | source)
XLA Modules:
  0.0 47.1 jit_solution(15057857350862233826)
XLA Ops:
  0.6 4.9 %shard_map.41 = (f32[512,2048]{1,0:T(8,128)S(1)}, f32[16,128]{1,0:T(8,128)S(1)}, f32[16,128]{1,0:T(8,128)S(1)}, bf16[2048,1024]{1,0:T(8,128)(2,1)S(1)}, bf16[512,256]{1,0:T(8,128)(2,1)S(1)}) custom-call(bf16[2048,1024]{1,0:T(8,128)(2,1)} %emb_hbm.1, bf16[512,1024]{1,0:T(8,128)(2,1)} %cent_hbm.1), custom_call_target="tpu_custom_call" | custom-call | tf_op jit(solution)/shard_map/pallas_call | solution.py:131
  5.5 0.1 collective-permute-start
  5.6 1.2 %collective-permute-done = f32[16,128]{1,0:T(8,128)S(1)} collective-permute-done((f32[16,128]{1,0:T(8,128)S(1)}, f32[16,128]{1,0:T(8,128)S(1)}, u32[]{:S(2)}, u32[]{:S(2)}) %collective-permute-start) | collective-permute-done | bytes 8224 | tf_op jit(solution)/shard_map/ppermute | solution.py:150
  6.8 23.5 %all_to_all.5.every_ref = f32[32,16,128]{2,1,0:T(8,128)S(1)} all-to-all(f32[32,16,128]{2,1,0:T(8,128)S(1)} %broadcast_in_dim.3), channel_id=1, replica_groups=mesh['x'=4,'z_hi'=4,'z_lo'=2,'y'=4,'core'=2] {'y','z_lo','z_hi'}, dimensions={0} | all-to-all | bytes 524288 | tf_op jit(solution)/shard_map/all_to_all | solution.py:154
  30.3 1.5 %shard_map.42 = (bf16[528,256]{1,0:T(8,128)(2,1)S(1)}, bf16[512,2048]{1,0:T(8,128)(2,1)S(1)}, bf16[16,256]{1,0:T(8,128)(2,1)S(1)}, f32[16,128]{1,0:T(8,128)}) custom-call(f32[512,2048]{1,0:T(8,128)S(1)} %get-tuple-element.15.p_ref, f32[16,128]{1,0:T(8,128)S(1)} %get-tuple-element.16.top_ref, f32[32,16,128]{2,1,0:T(8,128)S(1)} %all_to_all.5.every_ref, ...), custom_call_target="tpu_custom_call" | custom-call | tf_op jit(solution)/shard_map/pallas_call | solution.py:159
  31.8 1.4 %collective-permute-start.1 = (bf16[528,256]{1,0:T(8,128)(2,1)S(1)}, bf16[528,256]{1,0:T(8,128)(2,1)S(1)}, u32[]{:S(2)}, u32[]{:S(2)}) collective-permute-start(bf16[528,256]{1,0:T(8,128)(2,1)S(1)} %get-tuple-element.22), channel_id=1, source_target_pairs={{0,128},{64,192},{128,0},{192,64},{1,129},{65,193},{129,1},{193,65... | collective-permute-start | bytes 811016 | tf_op jit(solution)/shard_map/ppermute | solution.py:173
  33.2 1.3 %shard_map.44 = (bf16[528,256]{1,0:T(8,128)(2,1)S(1)}, bf16[528,256]{1,0:T(8,128)(2,1)S(1)}) custom-call(bf16[512,2048]{1,0:T(8,128)(2,1)S(1)} %get-tuple-element.19.w_ref, bf16[2048,1024]{1,0:T(8,128)(2,1)S(1)} %get-tuple-element.18.emb_ref, bf16[16,256]{1,0:T(8,128)(2,1)S(1)} %get-tuple-element.21.mass_ref), custom_call_target="tpu_custom_call" | custom-call | tf_op jit(solution)/shard_map/pallas_call | solution.py:175
  34.5 2.2 %collective-permute-start.2 = (bf16[528,256]{1,0:T(8,128)(2,1)S(1)}, bf16[528,256]{1,0:T(8,128)(2,1)S(1)}, u32[]{:S(2)}, u32[]{:S(2)}) collective-permute-start(bf16[528,256]{1,0:T(8,128)(2,1)S(1)} %get-tuple-element.25), channel_id=1, source_target_pairs={{0,64},{64,128},{128,192},{192,0},{1,65},{65,129},{129,193},{193,1... | collective-permute-start | bytes 811016 | tf_op jit(solution)/shard_map/ppermute | solution.py:173
  36.6 0.0 collective-permute-start.3
  36.6 6.1 %collective-permute-done.1.far_ref = bf16[528,256]{1,0:T(8,128)(2,1)S(1)} collective-permute-done((bf16[528,256]{1,0:T(8,128)(2,1)S(1)}, bf16[528,256]{1,0:T(8,128)(2,1)S(1)}, u32[]{:S(2)}, u32[]{:S(2)}) %collective-permute-start.1) | collective-permute-done | bytes 270368 | tf_op jit(solution)/shard_map/ppermute | solution.py:173
  42.7 0.7 %shard_map.43 = (f32[512,256]{1,0:T(8,128)S(1)}, f32[16,256]{1,0:T(8,128)S(1)}) custom-call(bf16[512,2048]{1,0:T(8,128)(2,1)S(1)} %get-tuple-element.19.w_ref, bf16[2048,1024]{1,0:T(8,128)(2,1)S(1)} %get-tuple-element.18.emb_ref, bf16[512,256]{1,0:T(8,128)(2,1)S(1)} %get-tuple-element.20.prior_ref, bf16[16,256]{1,0:T(8,128)(2,1)S(1)} %get-tuple-element.21.mass_ref, ...), custom_call_target="tpu_custom_call" | custom-call | tf_op jit(solution)/shard_map/pallas_call | solution.py:182
  43.5 0.0 collective-permute-done.2.refs_0_
  43.5 2.7 %collective-permute-done.3.refs_1_ = bf16[528,256]{1,0:T(8,128)(2,1)S(1)} collective-permute-done((bf16[528,256]{1,0:T(8,128)(2,1)S(1)}, bf16[528,256]{1,0:T(8,128)(2,1)S(1)}, u32[]{:S(2)}, u32[]{:S(2)}) %collective-permute-start.3) | collective-permute-done | bytes 270368 | tf_op jit(solution)/shard_map/ppermute | solution.py:173
  46.2 0.9 %shard_map.45 = f32[512,256]{1,0:T(8,128)} custom-call(f32[512,256]{1,0:T(8,128)S(1)} %get-tuple-element.23.own_ref, f32[16,256]{1,0:T(8,128)S(1)} %get-tuple-element.24.mass_ref, bf16[528,256]{1,0:T(8,128)(2,1)S(1)} %collective-permute-done.2.refs_0_, bf16[528,256]{1,0:T(8,128)(2,1)S(1)} %collective-permute-done.3.refs_1_), custom_call_target="tpu_custom_call" | custom-call | tf_op jit(solution)/shard_map/pallas_call | solution.py:190
  (2 shorter events, 0.0 us)
Async XLA Ops:
  5.5 1.3 %collective-permute-start = (f32[16,128]{1,0:T(8,128)S(1)}, f32[16,128]{1,0:T(8,128)S(1)}, u32[]{:S(2)}, u32[]{:S(2)}) collective-permute-start(f32[16,128]{1,0:T(8,128)S(1)} %get-tuple-element.17), channel_id=1, source_target_pairs={{0,1},{1,0},{2,3},{3,2},{4,5},{5,4},{6,7},{7,6},{8,9},{9,8},{10,11... | collective-permute-start | bytes 24584 | tf_op jit(solution)/shard_map/ppermute | solution.py:150
  31.8 10.9 %collective-permute-start.1 = (bf16[528,256]{1,0:T(8,128)(2,1)S(1)}, bf16[528,256]{1,0:T(8,128)(2,1)S(1)}, u32[]{:S(2)}, u32[]{:S(2)}) collective-permute-start(bf16[528,256]{1,0:T(8,128)(2,1)S(1)} %get-tuple-element.22), channel_id=1, source_target_pairs={{0,128},{64,192},{128,0},{192,64},{1,129},{65,193},{129,1},{193,65... | collective-permute-start | bytes 811016 | tf_op jit(solution)/shard_map/ppermute | solution.py:173
  34.5 9.0 %collective-permute-start.2 = (bf16[528,256]{1,0:T(8,128)(2,1)S(1)}, bf16[528,256]{1,0:T(8,128)(2,1)S(1)}, u32[]{:S(2)}, u32[]{:S(2)}) collective-permute-start(bf16[528,256]{1,0:T(8,128)(2,1)S(1)} %get-tuple-element.25), channel_id=1, source_target_pairs={{0,64},{64,128},{128,192},{192,0},{1,65},{65,129},{129,193},{193,1... | collective-permute-start | bytes 811016 | tf_op jit(solution)/shard_map/ppermute | solution.py:173
  36.6 9.5 %collective-permute-start.3 = (bf16[528,256]{1,0:T(8,128)(2,1)S(1)}, bf16[528,256]{1,0:T(8,128)(2,1)S(1)}, u32[]{:S(2)}, u32[]{:S(2)}) collective-permute-start(bf16[528,256]{1,0:T(8,128)(2,1)S(1)} %get-tuple-element.26), channel_id=1, source_target_pairs={{0,192},{64,0},{128,64},{192,128},{1,193},{65,1},{129,65},{193,129... | collective-permute-start | bytes 811016 | tf_op jit(solution)/shard_map/ppermute | solution.py:173

commit v9 on v8

--- a/solution.py
+++ b/solution.py
@@ -73,11 +73,15 @@
     totals = merge(every_ref[...])
     log_totals_ref[...] = totals * LN2
     factor = jnp.exp2(top_ref[...] - totals)
-    mass = jnp.zeros((cents, LANES), jnp.float32)
-    for k in range(rows // LANES):
-        w = p_ref[:, k * LANES : (k + 1) * LANES] * factor[k : k + 1, :]
-        w_ref[:, k * LANES : (k + 1) * LANES] = w.astype(jnp.bfloat16)
-        mass = mass + w
+    masses = []
+    for c in range(0, cents, 64):
+        mass = jnp.zeros((64, LANES), jnp.float32)
+        for k in range(rows // LANES):
+            w = p_ref[c : c + 64, k * LANES : (k + 1) * LANES] * factor[k : k + 1, :]
+            w_ref[c : c + 64, k * LANES : (k + 1) * LANES] = w.astype(jnp.bfloat16)
+            mass = mass + w
+        masses.append(mass)
+    mass = jnp.concatenate(masses, axis=0)
     part_ref[:cents, :] = part_product(shift, w_ref, emb_ref).astype(jnp.bfloat16)
     mass = jnp.broadcast_to(jnp.sum(mass, axis=1, keepdims=True), (cents, LANES)).T
     half = MASS_ROWS // 2

time: 47.2 us -> 47.2 us (level)
  no operation moved by 1% of the time
where the time goes in v9:
time: 47.2 us; the launch traced here: 47.1 us
  blocking collectives  23.5 us (50%)
  waiting for transfers between devices  9.91 us (21%)
  Pallas kernels  9.28 us (20%)
  starting transfers between devices  3.69 us (8%)
  between operations  0.68 us (1%)
    all_to_all x1, blocking collectives, shards(): lax.all_to_all(jnp.broadcast_to(chip, (chips,) + chip.shape), EXCHANGE, 0...  23.5 us
    ppermute x3, waiting for transfers between devices, send(): return lax.ppermute(p, 'x', [(k, (k + shift) % n_dp) for k in range(n_dp)])  8.75 us
    pallas_call x1, Pallas kernels, shards(): pl.pallas_call(functools.partial(logits_kernel, scale), in_specs=[IN_HBM]...  4.85 us
    ppermute x3, starting transfers between devices, send(): return lax.ppermute(p, 'x', [(k, (k + shift) % n_dp) for k in range(n_dp)])  3.59 us
    pallas_call x1, Pallas kernels, shards(): pl.pallas_call(functools.partial(weights_kernel, first), in_specs=[IN_VME...  1.48 us
    pallas_call x1, Pallas kernels, shards(): pl.pallas_call(functools.partial(parts_kernel, others), in_specs=[IN_VMEM...  1.27 us
    ppermute x1, waiting for transfers between devices, shards(): other = lax.ppermute(lse, 'core', [(0, 1), (1, 0)])  1.16 us
  transfers between devices with their start and end apart: 4, of which 3 were waited for; matrix products, arithmetic and copies ran while one was open for 0% of the time, Pallas kernels for 4%

profile of v9, /device:TPU:38, one launch (start us, length us, event | category | flops | bytes accessed | tf_op | source)
XLA Modules:
  0.0 47.1 jit_solution(17569720011604083838)
XLA Ops:
  0.6 4.9 %shard_map.41 = (f32[512,2048]{1,0:T(8,128)S(1)}, f32[16,128]{1,0:T(8,128)S(1)}, f32[16,128]{1,0:T(8,128)S(1)}, bf16[2048,1024]{1,0:T(8,128)(2,1)S(1)}, bf16[512,256]{1,0:T(8,128)(2,1)S(1)}) custom-call(bf16[2048,1024]{1,0:T(8,128)(2,1)} %emb_hbm.1, bf16[512,1024]{1,0:T(8,128)(2,1)} %cent_hbm.1), custom_call_target="tpu_custom_call" | custom-call | tf_op jit(solution)/shard_map/pallas_call | solution.py:135
  5.5 0.1 collective-permute-start
  5.6 1.2 %collective-permute-done = f32[16,128]{1,0:T(8,128)S(1)} collective-permute-done((f32[16,128]{1,0:T(8,128)S(1)}, f32[16,128]{1,0:T(8,128)S(1)}, u32[]{:S(2)}, u32[]{:S(2)}) %collective-permute-start) | collective-permute-done | bytes 8224 | tf_op jit(solution)/shard_map/ppermute | solution.py:154
  6.8 23.5 %all_to_all.5.every_ref = f32[32,16,128]{2,1,0:T(8,128)S(1)} all-to-all(f32[32,16,128]{2,1,0:T(8,128)S(1)} %broadcast_in_dim.3), channel_id=1, replica_groups=mesh['x'=4,'z_hi'=4,'z_lo'=2,'y'=4,'core'=2] {'y','z_lo','z_hi'}, dimensions={0} | all-to-all | bytes 524288 | tf_op jit(solution)/shard_map/all_to_all | solution.py:158
  30.3 1.5 %shard_map.42 = (bf16[528,256]{1,0:T(8,128)(2,1)S(1)}, bf16[512,2048]{1,0:T(8,128)(2,1)S(1)}, bf16[16,256]{1,0:T(8,128)(2,1)S(1)}, f32[16,128]{1,0:T(8,128)}) custom-call(f32[512,2048]{1,0:T(8,128)S(1)} %get-tuple-element.15.p_ref, f32[16,128]{1,0:T(8,128)S(1)} %get-tuple-element.16.top_ref, f32[32,16,128]{2,1,0:T(8,128)S(1)} %all_to_all.5.every_ref, ...), custom_call_target="tpu_custom_call" | custom-call | tf_op jit(solution)/shard_map/pallas_call | solution.py:163
  31.8 1.4 %collective-permute-start.1 = (bf16[528,256]{1,0:T(8,128)(2,1)S(1)}, bf16[528,256]{1,0:T(8,128)(2,1)S(1)}, u32[]{:S(2)}, u32[]{:S(2)}) collective-permute-start(bf16[528,256]{1,0:T(8,128)(2,1)S(1)} %get-tuple-element.22), channel_id=1, source_target_pairs={{0,128},{64,192},{128,0},{192,64},{1,129},{65,193},{129,1},{193,65... | collective-permute-start | bytes 811016 | tf_op jit(solution)/shard_map/ppermute | solution.py:177
  33.2 1.3 %shard_map.44 = (bf16[528,256]{1,0:T(8,128)(2,1)S(1)}, bf16[528,256]{1,0:T(8,128)(2,1)S(1)}) custom-call(bf16[512,2048]{1,0:T(8,128)(2,1)S(1)} %get-tuple-element.19.w_ref, bf16[2048,1024]{1,0:T(8,128)(2,1)S(1)} %get-tuple-element.18.emb_ref, bf16[16,256]{1,0:T(8,128)(2,1)S(1)} %get-tuple-element.21.mass_ref), custom_call_target="tpu_custom_call" | custom-call | tf_op jit(solution)/shard_map/pallas_call | solution.py:179
  34.5 2.2 %collective-permute-start.2 = (bf16[528,256]{1,0:T(8,128)(2,1)S(1)}, bf16[528,256]{1,0:T(8,128)(2,1)S(1)}, u32[]{:S(2)}, u32[]{:S(2)}) collective-permute-start(bf16[528,256]{1,0:T(8,128)(2,1)S(1)} %get-tuple-element.25), channel_id=1, source_target_pairs={{0,64},{64,128},{128,192},{192,0},{1,65},{65,129},{129,193},{193,1... | collective-permute-start | bytes 811016 | tf_op jit(solution)/shard_map/ppermute | solution.py:177
  36.6 0.0 collective-permute-start.3
  36.6 6.1 %collective-permute-done.1.far_ref = bf16[528,256]{1,0:T(8,128)(2,1)S(1)} collective-permute-done((bf16[528,256]{1,0:T(8,128)(2,1)S(1)}, bf16[528,256]{1,0:T(8,128)(2,1)S(1)}, u32[]{:S(2)}, u32[]{:S(2)}) %collective-permute-start.1) | collective-permute-done | bytes 270368 | tf_op jit(solution)/shard_map/ppermute | solution.py:177
  42.7 0.7 %shard_map.43 = (f32[512,256]{1,0:T(8,128)S(1)}, f32[16,256]{1,0:T(8,128)S(1)}) custom-call(bf16[512,2048]{1,0:T(8,128)(2,1)S(1)} %get-tuple-element.19.w_ref, bf16[2048,1024]{1,0:T(8,128)(2,1)S(1)} %get-tuple-element.18.emb_ref, bf16[512,256]{1,0:T(8,128)(2,1)S(1)} %get-tuple-element.20.prior_ref, bf16[16,256]{1,0:T(8,128)(2,1)S(1)} %get-tuple-element.21.mass_ref, ...), custom_call_target="tpu_custom_call" | custom-call | tf_op jit(solution)/shard_map/pallas_call | solution.py:186
  43.5 0.0 collective-permute-done.2.refs_0_
  43.5 2.7 %collective-permute-done.3.refs_1_ = bf16[528,256]{1,0:T(8,128)(2,1)S(1)} collective-permute-done((bf16[528,256]{1,0:T(8,128)(2,1)S(1)}, bf16[528,256]{1,0:T(8,128)(2,1)S(1)}, u32[]{:S(2)}, u32[]{:S(2)}) %collective-permute-start.3) | collective-permute-done | bytes 270368 | tf_op jit(solution)/shard_map/ppermute | solution.py:177
  46.2 0.9 %shard_map.45 = f32[512,256]{1,0:T(8,128)} custom-call(f32[512,256]{1,0:T(8,128)S(1)} %get-tuple-element.23.own_ref, f32[16,256]{1,0:T(8,128)S(1)} %get-tuple-element.24.mass_ref, bf16[528,256]{1,0:T(8,128)(2,1)S(1)} %collective-permute-done.2.refs_0_, bf16[528,256]{1,0:T(8,128)(2,1)S(1)} %collective-permute-done.3.refs_1_), custom_call_target="tpu_custom_call" | custom-call | tf_op jit(solution)/shard_map/pallas_call | solution.py:194
  (2 shorter events, 0.0 us)
Async XLA Ops:
  5.5 1.3 %collective-permute-start = (f32[16,128]{1,0:T(8,128)S(1)}, f32[16,128]{1,0:T(8,128)S(1)}, u32[]{:S(2)}, u32[]{:S(2)}) collective-permute-start(f32[16,128]{1,0:T(8,128)S(1)} %get-tuple-element.17), channel_id=1, source_target_pairs={{0,1},{1,0},{2,3},{3,2},{4,5},{5,4},{6,7},{7,6},{8,9},{9,8},{10,11... | collective-permute-start | bytes 24584 | tf_op jit(solution)/shard_map/ppermute | solution.py:154
  31.8 10.9 %collective-permute-start.1 = (bf16[528,256]{1,0:T(8,128)(2,1)S(1)}, bf16[528,256]{1,0:T(8,128)(2,1)S(1)}, u32[]{:S(2)}, u32[]{:S(2)}) collective-permute-start(bf16[528,256]{1,0:T(8,128)(2,1)S(1)} %get-tuple-element.22), channel_id=1, source_target_pairs={{0,128},{64,192},{128,0},{192,64},{1,129},{65,193},{129,1},{193,65... | collective-permute-start | bytes 811016 | tf_op jit(solution)/shard_map/ppermute | solution.py:177
  34.5 9.0 %collective-permute-start.2 = (bf16[528,256]{1,0:T(8,128)(2,1)S(1)}, bf16[528,256]{1,0:T(8,128)(2,1)S(1)}, u32[]{:S(2)}, u32[]{:S(2)}) collective-permute-start(bf16[528,256]{1,0:T(8,128)(2,1)S(1)} %get-tuple-element.25), channel_id=1, source_target_pairs={{0,64},{64,128},{128,192},{192,0},{1,65},{65,129},{129,193},{193,1... | collective-permute-start | bytes 811016 | tf_op jit(solution)/shard_map/ppermute | solution.py:177
  36.6 9.5 %collective-permute-start.3 = (bf16[528,256]{1,0:T(8,128)(2,1)S(1)}, bf16[528,256]{1,0:T(8,128)(2,1)S(1)}, u32[]{:S(2)}, u32[]{:S(2)}) collective-permute-start(bf16[528,256]{1,0:T(8,128)(2,1)S(1)} %get-tuple-element.26), channel_id=1, source_target_pairs={{0,192},{64,0},{128,64},{192,128},{1,193},{65,1},{129,65},{193,129... | collective-permute-start | bytes 811016 | tf_op jit(solution)/shard_map/ppermute | solution.py:177
